TPU v7x, 256 devices: a whole 4x4x8 slice. The times are simulated.
256 devices in a mesh: ctx: 4 (over z_hi), tp: 8 (over y, core), dec: 8 (over x, z_lo).
Axes of the slice: x: 4, y: 4, z: 8 (z_hi: 4, z_lo: 2; z = z_hi * 2 + z_lo), core: 2. Of those that a mesh axis runs over, the one named last changes fastest.
Arguments:
- cache: bfloat16 [8, 1024, 576], P('dec', 'ctx'), may hold values from -6 to 6
- lengths: int32 [8], P('dec'), may hold values from 1 to 1024
- slot_sequence: int32 [8], replicated, may hold values from 0 to 7, each once
- parents: int32 [8, 64], P('dec'), may hold values from 0 to 62, as said below
- query_nope: bfloat16 [8, 64, 128, 128], P('dec', None, 'tp'), may hold values from -6 to 6
- query_rope: bfloat16 [8, 64, 128, 64], P('dec', None, 'tp'), may hold values from -90 to 90
- new_latent: bfloat16 [8, 64, 576], P('dec'), may hold values from -6 to 6
- key_up: bfloat16 [128, 128, 512], P('tp'), may hold values from -0.5 to 0.5
- value_up: bfloat16 [128, 512, 128], P('tp'), may hold values from -0.25 to 0.25
- out_proj: bfloat16 [16384, 7168], P('tp', ('ctx', 'dec')), may hold values from -0.046875 to 0.046875
Outputs:
- attended: bfloat16 [8, 64, 7168], P(None, 'tp', ('ctx', 'dec'))
Inputs may be any that keep to these rules, and one draw needn't show every extreme that they name: `slot_sequence`: every sequence is held by exactly one slot. parents[s, 0] = 0 and parents[s, i] < i for every i >= 1.
All inputs are finite; a program needn't handle non-finite values.
Results may differ from a plain program's by a relative error of at most 0.024.
Values may be sent and summed in bfloat16 or wider, within the bound.
A program may use at most 64 MiB of HBM per device.

v0:
```python
import math

import jax
import jax.numpy as jnp
from jax import lax
from jax.sharding import PartitionSpec as P


def joined_along(blocks, dim):
    shape = list(blocks.shape[1:])
    shape[dim] *= blocks.shape[0]
    return jnp.moveaxis(blocks, 0, dim).reshape(shape)


def sent_to_all(value, axis):
    copies = jnp.broadcast_to(value, (lax.axis_size(axis), *value.shape))
    return lax.all_to_all(copies, axis, split_axis=0, concat_axis=0, tiled=True)


def collect(value, axis, dim):
    return joined_along(sent_to_all(value, axis), dim)


def sent_together(arrays, axis, dim, along):
    columns = [a.reshape(*a.shape[:along], -1) for a in arrays]
    both = jnp.concatenate(columns, axis=along)
    whole, at, done = (collect(both, axis, dim), 0, [])
    for a, column in zip(arrays, columns):
        piece = whole[..., at : at + column.shape[along]]
        done.append(piece.reshape(*piece.shape[:along], *a.shape[along:]))
        at += column.shape[along]
    return tuple(done)


def for_sending(value):

    def short(part):
        return part.astype(jnp.bfloat16) if part.dtype == jnp.float32 else part

    return jax.tree.map(short, value)


def in_blocks(value, dim, size):
    before, after = (value.shape[:dim], value.shape[dim + 1 :])
    return jnp.moveaxis(value.reshape(*before, size, -1, *after), dim, 0)


def sent_and_summed(value, axis, dim):
    size = lax.axis_size(axis)
    blocks = lax.all_to_all(in_blocks(value, dim, size), axis, 0, 0, tiled=True)
    return jnp.sum(blocks.astype(jnp.float32), axis=0)


def ancestors(parents):
    node_count = parents.shape[-1]
    node_ids = jnp.arange(node_count, dtype=jnp.int32)
    parent_link = (parents[..., :, None] == node_ids).astype(jnp.float32)
    closure = jnp.maximum(parent_link, jnp.eye(node_count, dtype=jnp.float32))
    for _ in range(node_count.bit_length()):
        closure = jnp.minimum(
            jnp.einsum("sij,sjk->sik", closure, closure, precision=lax.Precision.HIGHEST), 1.0
        )
    return closure


def partial_softmax(queries, key_rows, live_mask, latent, score_scale):
    scores = (
        jnp.einsum("snhc,spc->snhp", queries, key_rows, preferred_element_type=jnp.float32)
        * score_scale
    )
    alive = live_mask > 0
    scores = jnp.where(alive, scores, -1e30)
    row_peak = jnp.max(scores, axis=-1)
    expo = jnp.where(alive, jnp.exp(scores - row_peak[..., None]), 0.0)
    row_total = jnp.sum(expo, axis=-1)
    weighted = jnp.einsum(
        "snhp,spc->snhc",
        expo.astype(jnp.bfloat16),
        key_rows[..., :latent],
        preferred_element_type=jnp.float32,
    )
    return (row_peak, row_total, weighted)


def join_parts(first_part, second_part):
    new_peak = jnp.maximum(first_part[0], second_part[0])
    first_factor = jnp.exp(first_part[0] - new_peak)
    second_factor = jnp.exp(second_part[0] - new_peak)
    row_total = first_part[1] * first_factor + second_part[1] * second_factor
    weighted = first_part[2] * first_factor[..., None] + second_part[2] * second_factor[..., None]
    return (new_peak, row_total, weighted)


def pick_rows(select, pieces):
    flat_rows = pieces.reshape(pieces.shape[0], -1)
    chosen = jnp.dot(select, flat_rows, preferred_element_type=jnp.float32)
    return chosen.reshape((select.shape[0],) + pieces.shape[1:]).astype(pieces.dtype)


def to_values(part, value_weight):
    projected = jnp.einsum("snhc,hcv->snhv", part[2], value_weight, precision=lax.Precision.HIGHEST)
    return (part[0], part[1], projected)


def on_device(
    cache,
    lengths,
    slot_sequence,
    parents,
    query_nope,
    query_rope,
    new_latent,
    key_up,
    value_up,
    out_proj,
):
    seq_dev = cache.shape[0]
    ctx_len = cache.shape[1]
    latent = value_up.shape[1]
    node_count = parents.shape[1]
    ctx_count = lax.axis_size("ctx")
    dec_count = lax.axis_size("dec")
    ctx_at = lax.axis_index("ctx")
    dec_at = lax.axis_index("dec")
    score_scale = 1.0 / math.sqrt(key_up.shape[1] + cache.shape[2] - latent)
    positions = ctx_at * ctx_len + jnp.arange(ctx_len, dtype=jnp.int32)
    valid = (positions[None, :] < lengths[:, None]).astype(jnp.bfloat16)
    tree_local = ancestors(parents).astype(jnp.bfloat16)
    value_weight = value_up.astype(jnp.float32)
    wanted = lax.dynamic_slice_in_dim(slot_sequence, dec_at * seq_dev, seq_dev)
    pieces = sent_together((cache, valid), "dec", 0, 2)
    piece_count = pieces[0].shape[0]
    sources = jnp.arange(piece_count, dtype=jnp.int32)
    select = (wanted[:, None] == sources[None, :]).astype(jnp.bfloat16)
    key_rows = pick_rows(select, pieces[0])
    live_rows = pick_rows(select, pieces[1])
    nope_rows, rope_rows, tree_keys, tree_mask = (query_nope, query_rope, new_latent, tree_local)
    absorbed = jnp.einsum(
        "snhd,hdc->snhc", nope_rows, key_up, preferred_element_type=jnp.float32
    ).astype(jnp.bfloat16)
    queries = jnp.concatenate([absorbed, rope_rows], axis=-1)
    cache_part = partial_softmax(
        queries, key_rows, live_rows[:, None, None, :], latent, score_scale
    )
    cache_part = to_values(cache_part, value_weight)
    node_block = node_count // ctx_count
    first_node = ctx_at * node_block
    stacked = tuple((member[None] for member in cache_part))
    spread = jax.tree.map(
        lambda part, own: part.astype(own.dtype),
        lax.all_to_all(for_sending(stacked), "ctx", split_axis=2, concat_axis=0, tiled=True),
        stacked,
    )
    peak_all = jnp.max(spread[0], axis=0)
    factors = jnp.exp(spread[0] - peak_all[None])
    merged = (
        peak_all,
        jnp.sum(spread[1] * factors, axis=0),
        jnp.sum(spread[2] * factors[..., None], axis=0),
    )
    block_queries = lax.dynamic_slice_in_dim(queries, first_node, node_block, 1)
    block_tree = lax.dynamic_slice_in_dim(tree_mask, first_node, node_block, 1)
    tree_part = partial_softmax(
        block_queries, tree_keys, block_tree[:, :, None, :], latent, score_scale
    )
    tree_part = to_values(tree_part, value_weight)
    final = join_parts(merged, tree_part)
    head_values = (final[2] / final[1][..., None]).astype(jnp.bfloat16)
    head_values = head_values.reshape(seq_dev, node_block, -1)
    projected = jnp.einsum(
        "ksnv,vd->ksnd",
        lax.all_gather(head_values[None], ("ctx", "dec"), axis=0, tiled=True),
        out_proj,
        preferred_element_type=jnp.float32,
    )
    column_count = out_proj.shape[1]
    projected = projected.reshape(ctx_count, dec_count, seq_dev, node_block, column_count)
    projected = projected.transpose(1, 2, 0, 3, 4).reshape(
        dec_count * seq_dev, node_count, column_count
    )
    return sent_and_summed(projected.astype(jnp.bfloat16), "tp", 1).astype(jnp.bfloat16)


def solution(mesh):
    return jax.shard_map(
        on_device,
        mesh=mesh,
        in_specs=(
            P("dec", "ctx", None),
            P("dec"),
            P(),
            P("dec", None),
            P("dec", None, "tp", None),
            P("dec", None, "tp", None),
            P("dec", None, None),
            P("tp", None, None),
            P("tp", None, None),
            P("tp", ("ctx", "dec")),
        ),
        out_specs=P(None, "tp", ("ctx", "dec")),
        check_vma=False,
    )
```

profile of v0, /device:TPU:1, one launch (start us, length us, event | category | flops | bytes accessed | tf_op | source)
XLA Modules:
  0.0 289.7 jit_solution(6729289213615725984)
XLA Ops:
  8.3 1.6 broadcast_in_dim.58
  9.9 6.3 %all-to-all-start = ((bf16[8,1,256,577]{2,3,1,0:T(8,128)(2,1)}), bf16[8,1,256,577]{2,3,1,0:T(8,128)(2,1)}, u32[]{:S(2)}, u32[]{:S(2)}) async-start(bf16[8,1,256,577]{2,3,1,0:T(8,128)(2,1)} %broadcast_in_dim.58), calls=%async_computation | async-start | bytes 4784128 | tf_op jit(solution)/shard_map/all_to_all | solution.py:17
  17.7 1.4 fusion.2
  20.8 1.7 fusion.30
  27.7 17.5 %all-to-all-done = bf16[8,1,256,577]{2,3,1,0:T(8,128)(2,1)} async-done(((bf16[8,1,256,577]{2,3,1,0:T(8,128)(2,1)}), bf16[8,1,256,577]{2,3,1,0:T(8,128)(2,1)}, u32[]{:S(2)}, u32[]{:S(2)}) %all-to-all-start) | async-done | bytes 2363424 | tf_op jit(solution)/shard_map/all_to_all | solution.py:17
  45.2 2.2 copy.165
  48.1 1.6 slice.17
  49.7 4.8 %copy.118 = bf16[8,256,576]{2,1,0:T(8,128)(2,1)} copy(bf16[8,256,576]{1,0,2:T(8,128)(2,1)} %slice.17) | data formatting | bytes 4718592 | tf_op jit(solution)/shard_map/slice | solution.py:29
  54.5 5.8 %reshape.529 = bf16[1179648]{0:T(1024)(128)(2,1)} reshape(bf16[8,256,576]{2,1,0:T(8,128)(2,1)} %copy.118) | data formatting | bytes 4718592
  60.4 4.1 %reshape.511 = bf16[8,147456]{1,0:T(8,128)(2,1)} reshape(bf16[1179648]{0:T(1024)(128)(2,1)} %reshape.529) | data formatting | bytes 4718592 | tf_op jit(solution)/shard_map/reshape | solution.py:95
  64.4 4.2 %reshape.531 = bf16[1179648]{0:T(1024)(128)(2,1)} reshape(bf16[8,147456]{1,0:T(8,128)(2,1)} %reshape.511) | data formatting | bytes 4718592
  68.6 5.5 %reshape.532 = bf16[8,256,576]{2,1,0:T(8,128)(2,1)} reshape(bf16[1179648]{0:T(1024)(128)(2,1)} %reshape.531) | data formatting | bytes 4718592
  74.1 2.5 multiply_reduce_fusion
  76.6 2.0 fusion.50
  78.7 1.6 fusion.19
  82.4 7.7 %all-to-all-start.2 = ((bf16[4,2,128]{2,1,0:T(2,128)(2,1)}), bf16[4,2,128]{2,1,0:T(2,128)(2,1)S(1)}, u32[]{:S(2)}, u32[]{:S(2)}) async-start(bf16[4,2,128]{2,1,0:T(2,128)(2,1)} %reshape.533), calls=%async_computation.2 | async-start | bytes 4096 | tf_op jit(solution)/shard_map/all_to_all | solution.py:151
  96.6 5.5 %all-to-all-start.3 = ((bf16[4,2,128]{2,1,0:T(2,128)(2,1)}), bf16[4,2,128]{2,1,0:T(2,128)(2,1)S(1)}, u32[]{:S(2)}, u32[]{:S(2)}) async-start(bf16[4,2,128]{2,1,0:T(2,128)(2,1)} %reshape.535), calls=%async_computation.3 | async-start | bytes 4096 | tf_op jit(solution)/shard_map/all_to_all | solution.py:151
  102.5 6.0 %all-to-all-done.3 = bf16[4,2,128]{2,1,0:T(2,128)(2,1)S(1)} async-done(((bf16[4,2,128]{2,1,0:T(2,128)(2,1)}), bf16[4,2,128]{2,1,0:T(2,128)(2,1)S(1)}, u32[]{:S(2)}, u32[]{:S(2)}) %all-to-all-start.3) | async-done | bytes 2080 | tf_op jit(solution)/shard_map/all_to_all | solution.py:151
  108.5 3.4 %all-to-all-start.1 = ((bf16[1,1,64,16,128]{4,3,1,0,2:T(8,128)(2,1)}), bf16[1,1,64,16,128]{4,3,1,0,2:T(8,128)(2,1)S(1)}, u32[]{:S(2)}, u32[]{:S(2)}) async-start(bf16[1,1,64,16,128]{4,3,1,0,2:T(8,128)(2,1)} %copy.122), calls=%async_computation.1 | async-start | bytes 524288 | tf_op jit(solution)/shard_map/all_to_all | solution.py:151
  112.4 7.5 %all-to-all-done.1 = bf16[1,1,64,16,128]{4,3,1,0,2:T(8,128)(2,1)S(1)} async-done(((bf16[1,1,64,16,128]{4,3,1,0,2:T(8,128)(2,1)}), bf16[1,1,64,16,128]{4,3,1,0,2:T(8,128)(2,1)S(1)}, u32[]{:S(2)}, u32[]{:S(2)}) %all-to-all-start.1) | async-done | bytes 262176 | tf_op jit(solution)/shard_map/all_to_all | solution.py:151
  120.1 2.5 fusion.17
  123.4 126.0 %all-gather.2.cloned.1.call-done = bf16[32,1,16,2048]{3,2,1,0:T(8,128)(2,1)} async-done(((bf16[1,1,16,2048]{3,2,1,0:T(8,128)(2,1)}), bf16[32,1,16,2048]{3,2,1,0:T(8,128)(2,1)}) %all-gather.2.cloned.1.call-update) | async-done | bytes 2097168 | tf_op jit(solution)/shard_map/all_gather | solution.py:172
  249.4 2.5 fusion.9
  252.0 30.2 %all_to_all.40 = bf16[8,8,8,224]{3,2,1,0:T(8,128)(2,1)S(1)} all-to-all(bf16[8,8,8,224]{3,2,1,0:T(8,128)(2,1)S(1)} %copy.139), channel_id=1, replica_groups=mesh['ctx'=4,'tp'=8,'dec'=8] {'tp'}, dimensions={0} | all-to-all | bytes 458752 | tf_op jit(solution)/shard_map/all_to_all | solution.py:50
  (79 shorter events, 21.0 us)
Async XLA Ops:
  6.5 11.2 %copy-start = (bf16[16,128,512]{2,1,0:T(8,128)(2,1)S(1)}, bf16[16,128,512]{2,1,0:T(8,128)(2,1)}, u32[]{:S(2)}) copy-start(bf16[16,128,512]{2,1,0:T(8,128)(2,1)} %param.17) | copy-start | bytes 6291460
  9.9 6.3 %copy-start.3 = (bf16[1,64,16,64]{3,2,1,0:T(8,128)(2,1)S(1)}, bf16[1,64,16,64]{3,2,1,0:T(8,128)(2,1)}, u32[]{:S(2)}) copy-start(bf16[1,64,16,64]{3,2,1,0:T(8,128)(2,1)} %param.15) | copy-start | bytes 393220
  9.9 6.4 %copy-start.9 = (s32[1,64]{1,0:T(1,128)S(1)}, s32[1,64]{1,0:T(1,128)}, u32[]{:S(2)}) copy-start(s32[1,64]{1,0:T(1,128)} %param.13) | copy-start | bytes 772
  9.9 35.3 %all-to-all-start = ((bf16[8,1,256,577]{2,3,1,0:T(8,128)(2,1)}), bf16[8,1,256,577]{2,3,1,0:T(8,128)(2,1)}, u32[]{:S(2)}, u32[]{:S(2)}) async-start(bf16[8,1,256,577]{2,3,1,0:T(8,128)(2,1)} %broadcast_in_dim.58), calls=%async_computation | async-start | bytes 4784128 | tf_op jit(solution)/shard_map/all_to_all | solution.py:17
  17.7 1.5 copy-start.8
  17.7 1.5 copy-start.4
  20.1 0.7 copy-start.7
  68.6 5.5 %copy-start.10 = (f32[8]{0:T(128)S(1)}, f32[8]{0:T(128)}, u32[]{:S(2)}) copy-start(f32[8]{0:T(128)} %bitcast_convert_fusion) | copy-start | bytes 100
  74.1 2.5 copy-start.2
  82.4 14.2 %all-to-all-start.2 = ((bf16[4,2,128]{2,1,0:T(2,128)(2,1)}), bf16[4,2,128]{2,1,0:T(2,128)(2,1)S(1)}, u32[]{:S(2)}, u32[]{:S(2)}) async-start(bf16[4,2,128]{2,1,0:T(2,128)(2,1)} %reshape.533), calls=%async_computation.2 | async-start | bytes 4096 | tf_op jit(solution)/shard_map/all_to_all | solution.py:151
  90.1 1.6 copy-start.1
  91.7 20.7 %copy-start.5 = (f32[16,16]{0,1:T(8,128)S(1)}, f32[16,16]{0,1:T(8,128)}, u32[]{:S(2)}) copy-start(f32[16,16]{0,1:T(8,128)} %copy.129) | copy-start | bytes 3076
  91.7 20.7 %copy-start.6 = (f32[16,16]{0,1:T(8,128)S(1)}, f32[16,16]{0,1:T(8,128)}, u32[]{:S(2)}) copy-start(f32[16,16]{0,1:T(8,128)} %copy.136) | copy-start | bytes 3076
  96.6 11.9 %all-to-all-start.3 = ((bf16[4,2,128]{2,1,0:T(2,128)(2,1)}), bf16[4,2,128]{2,1,0:T(2,128)(2,1)S(1)}, u32[]{:S(2)}, u32[]{:S(2)}) async-start(bf16[4,2,128]{2,1,0:T(2,128)(2,1)} %reshape.535), calls=%async_computation.3 | async-start | bytes 4096 | tf_op jit(solution)/shard_map/all_to_all | solution.py:151
  108.5 11.4 %all-to-all-start.1 = ((bf16[1,1,64,16,128]{4,3,1,0,2:T(8,128)(2,1)}), bf16[1,1,64,16,128]{4,3,1,0,2:T(8,128)(2,1)S(1)}, u32[]{:S(2)}, u32[]{:S(2)}) async-start(bf16[1,1,64,16,128]{4,3,1,0,2:T(8,128)(2,1)} %copy.122), calls=%async_computation.1 | async-start | bytes 524288 | tf_op jit(solution)/shard_map/all_to_all | solution.py:151
  111.9 137.5 %all-gather.2.cloned.1.call-start = ((), (), s32[]{:S(2)}) async-start(), calls=%async_computation.5 | async-start | bytes 2162688 | tf_op jit(solution)/shard_map/all_gather | solution.py:172
Sparse Core Ops, SparseCore 0:
  123.5 125.8 all-gather.1
where the time goes:
time: 291 us; the launch traced here: 290 us
  waiting for transfers between devices  158 us (54%)
  local copies, waits for them, and re-layouts  38.7 us (13%)
  blocking collectives  30.2 us (10%)
  starting transfers between devices  23 us (8%)
  between operations  14.5 us (5%)
  matrix products  13.2 us (5%)
  other arithmetic  12 us (4%)
    all_gather x1, waiting for transfers between devices, on_device(): lax.all_gather(head_values[None], ('ctx', 'dec'), axis=0, tiled=True)  126 us
    all_to_all x1, blocking collectives, sent_and_summed(): blocks = lax.all_to_all(in_blocks(value, dim, size), axis, 0, 0, tiled=True)  30.2 us
    unnamed x31, local copies, waits for them, and re-layouts  18.9 us
    all_to_all x1, waiting for transfers between devices, sent_to_all(): return lax.all_to_all(copies, axis, split_axis=0, concat_axis=0, tiled=True)  17.5 us
    all_to_all x3, starting transfers between devices, on_device(): lax.all_to_all(for_sending(stacked), 'ctx', split_axis=2, concat_axis=0,...  16.6 us
    all_to_all x3, waiting for transfers between devices, on_device(): lax.all_to_all(for_sending(stacked), 'ctx', split_axis=2, concat_axis=0,...  14.7 us
    slice x2, local copies, waits for them, and re-layouts, sent_together(): piece = whole[..., at:at + column.shape[along]]  6.41 us
    all_to_all x1, starting transfers between devices, sent_to_all(): return lax.all_to_all(copies, axis, split_axis=0, concat_axis=0, tiled=True)  6.33 us
  transfers between devices with their start and end apart: 5, of which 5 were waited for; matrix products, arithmetic and copies ran while one was open for 6% of the time, Pallas kernels for 0%

commit v1 on v0

v1 whole, which is shorter than its diff:
```python
import math

import jax
import jax.numpy as jnp
from jax import lax
from jax.experimental import pallas as pl
from jax.experimental.pallas import tpu as pltpu
from jax.sharding import PartitionSpec as P

MESH = pl.DeviceIdType.MESH
F32 = jnp.float32
BF16 = jnp.bfloat16
GROUPS = 2
DEAD = -1e30


def nt_dot(a, b):
    return lax.dot_general(a, b, (((1,), (1,)), ((), ())), preferred_element_type=F32)


def nn_dot(a, b):
    return jnp.dot(a, b, preferred_element_type=F32)


def permuted(source_of, value):
    rows = value.shape[0]
    r = lax.broadcasted_iota(jnp.int32, (rows, rows), 0)
    s = lax.broadcasted_iota(jnp.int32, (rows, rows), 1)
    select = jnp.where(source_of(r) == s, 1.0, 0.0).astype(BF16)
    return nn_dot(select, value).astype(BF16)


def kernel(
    cache_ref, length_ref, slot_ref, parents_ref, nope_ref, rope_ref, latent_ref, key_up_ref, value_up_ref, proj_ref,
    out_ref,
    raw, live, keys, nope, rope, tree_rows, key_up, value_up, proj, queries, heads, partial, sums,
    local_sem, raw_sem, live_sem, key_sem, a_sem, b_sem, sum_sem, send_sem,
):
    ctx, tp, dec = lax.axis_index("ctx"), lax.axis_index("tp"), lax.axis_index("dec")
    x, z_lo = dec // 2, dec % 2
    y, core = tp // 2, tp % 2
    z = ctx * 2 + z_lo
    nodes, head_count = 16, 16
    scale = 1.0 / math.sqrt(192.0)

    def at_x(dx, dz=0):
        xx, zz = (x + dx + 4) % 4, (z + dz + 8) % 8
        return (zz // 2, tp, xx * 2 + zz % 2)

    def at_tp(dy, other_core=False):
        core_there = 1 - core if other_core else core
        return (ctx, ((y + dy) % 4) * 2 + core_there, dec)

    def at_dec(k):
        return (ctx, tp, (dec + k) % 8)

    def at_ctx(k):
        return ((ctx + k) % 4, tp, dec)

    peers = [at_dec(k) for k in range(1, 8)]
    peers += [at_ctx(k) for k in range(1, 4)]
    peers += [at_tp(dy) for dy in (1, 2, 3)] + [at_tp(dy, True) for dy in range(4)]
    away = (z + 7 + 2 * z_lo) % 8
    peers.append((away // 2, tp, x * 2 + away % 2))

    started = []

    def send(src, dst, sem, device):
        copy = pltpu.make_async_remote_copy(
            src_ref=src, dst_ref=dst, send_sem=send_sem.at[len(started)], recv_sem=sem,
            device_id=device, device_id_type=MESH,
        )
        copy.start()
        started.append(copy)

    def arrived(dst, sem):
        pltpu.make_async_remote_copy(
            src_ref=dst, dst_ref=dst, send_sem=send_sem.at[0], recv_sem=sem,
            device_id=at_dec(1), device_id_type=MESH,
        ).wait_recv()

    loads = []

    def load(src, dst):
        copy = pltpu.make_async_copy(src, dst, local_sem.at[len(loads)])
        copy.start()
        loads.append(copy)
        return copy

    own_rows = cache_ref.at[pl.ds(pl.multiple_of(tp * 32, 32), 32)]
    load_raw = load(own_rows, raw.at[dec])
    load_nope = load(nope_ref.at[:, pl.ds(ctx * 2, 2)], nope)
    load_rope = load(rope_ref.at[:, pl.ds(ctx * 2, 2)], rope)
    load_tree = load(latent_ref, tree_rows)
    load_key_up = load(key_up_ref, key_up)
    load_value_up = load(value_up_ref, value_up)
    load_proj = load(proj_ref, proj)

    live[dec] = jnp.full((8, 128), length_ref[0], jnp.int32)

    barrier = pltpu.get_barrier_semaphore()
    for peer in peers:
        pl.semaphore_signal(barrier, inc=1, device_id=peer, device_id_type=MESH)
    pl.semaphore_wait(barrier, len(peers))

    for k in range(1, 8):
        send(live.at[dec], live.at[dec], live_sem.at[dec], at_dec(k))
        send(own_rows, raw.at[dec], raw_sem.at[dec], at_dec(k))

    j_at = lax.broadcasted_iota(jnp.int32, (64, 64), 0)
    i_at = lax.broadcasted_iota(jnp.int32, (64, 64), 1)
    closure = jnp.where((parents_ref[...] == j_at) | (i_at == j_at), 1.0, 0.0)
    for _ in range(6):
        closure = jnp.minimum(nn_dot(closure.astype(BF16), closure.astype(BF16)), 1.0)
    row = lax.broadcasted_iota(jnp.int32, (128, 64), 0) % 16
    own_node = lax.broadcasted_iota(jnp.int32, (128, 64), 1) == 8 * (row // 2) + 2 * ctx + row % 2
    on_path = nt_dot(jnp.where(own_node, 1.0, 0.0).astype(BF16), closure.astype(BF16))
    tree_bias = (on_path - 1.0) * 1e30

    def by_head(r):
        return (r % 16) * 16 + r // 16

    load_nope.wait()
    load_rope.wait()
    nope_rows = permuted(by_head, nope[...].reshape(256, 128))
    rope_rows = permuted(by_head, rope[...].reshape(256, 64))
    lane = lax.broadcasted_iota(jnp.int32, (256, 64), 1)
    queries[:, 512:640] = jnp.concatenate([rope_rows, jnp.where(lane == 0, 1.0, 0.0).astype(BF16)], axis=1)
    load_key_up.wait()
    for h in range(head_count):
        rows = slice(h * nodes, (h + 1) * nodes)
        queries[rows, 0:512] = nn_dot(nope_rows[rows], key_up[h]).astype(BF16)

    load_raw.wait()
    for k in range(1, 8):
        source = (dec + k) % 8
        arrived(live.at[source], live_sem.at[source])
        arrived(raw.at[source], raw_sem.at[source])
    wanted = slot_ref[dec]
    position = ctx * 256 + tp * 32 + lax.broadcasted_iota(jnp.int32, (32, 64), 0)
    first_lane = lax.broadcasted_iota(jnp.int32, (32, 64), 1) == 0
    dead = (position >= live[wanted][0:1, 0:64]) & first_lane
    keys[ctx * 8 + tp] = jnp.concatenate([raw[wanted], jnp.where(dead, DEAD, 0.0).astype(BF16)], axis=1)

    def pass_on(slot, device):
        send(keys.at[slot], keys.at[slot], key_sem.at[slot], device)

    own_slot = ctx * 8 + tp
    for k in (1, 3, 2):
        pass_on(own_slot, at_ctx(k))
    for k in (0, 1, 3, 2):
        slot = ((ctx + k) % 4) * 8 + tp
        if k:
            arrived(keys.at[slot], key_sem.at[slot])
        for dy in (1, 3, 2):
            pass_on(slot, at_tp(dy))
        pass_on(slot, at_tp(0, True))
    for k in (0, 1, 3, 2):
        for dy in (1, 3, 2):
            slot = ((ctx + k) % 4) * 8 + ((y + dy) % 4) * 2 + core
            arrived(keys.at[slot], key_sem.at[slot])
            pass_on(slot, at_tp(0, True))
    for k in (0, 1, 3, 2):
        for dy in (0, 1, 3, 2):
            slot = ((ctx + k) % 4) * 8 + ((y + dy) % 4) * 2 + 1 - core
            arrived(keys.at[slot], key_sem.at[slot])

    load_tree.wait()
    load_value_up.wait()

    group_heads = head_count // GROUPS
    group_rows = group_heads * nodes

    def attend(g):
        q = queries[g * group_rows : (g + 1) * group_rows, :]
        s = nt_dot(q, keys[...].reshape(1024, 640)) * scale
        s_tree = nt_dot(q[:, :576], tree_rows[...]) * scale + tree_bias[:group_rows]
        peak = jnp.maximum(jnp.max(s, axis=-1, keepdims=True), jnp.max(s_tree, axis=-1, keepdims=True))
        e = jnp.exp(s - peak)
        e_tree = jnp.exp(s_tree - peak)
        total = jnp.sum(e, axis=-1, keepdims=True) + jnp.sum(e_tree, axis=-1, keepdims=True)
        o = nn_dot(e.astype(BF16), keys[:, :, 0:512].reshape(1024, 512))
        o = o + nn_dot(e_tree.astype(BF16), tree_rows[:, 0:512])
        o = (o / total).astype(BF16)
        for h in range(group_heads):
            head = g * group_heads + h
            done = nn_dot(o[h * nodes : (h + 1) * nodes], value_up[head]).astype(BF16)
            heads[z * 4 + x, :, head * 128 : (head + 1) * 128] = done

    a_width = group_heads * 3 // 8 * 128
    b_width = group_heads * 128 - a_width

    def block(part, g, dx, dz):
        slot = ((z + dz + 8) % 8) * 4 + (x + dx + 4) % 4
        start = g * group_heads * 128 + (0 if part == 0 else a_width)
        ref = heads.at[slot, :, pl.ds(start, a_width if part == 0 else b_width)]
        return ref, (a_sem, b_sem)[part].at[g * 32 + slot]

    def relay(part, g, dx, dz, to_dx, to_dz):
        ref, sem = block(part, g, dx, dz)
        send(ref, ref, sem, at_x(to_dx, to_dz))

    def come(part, g, dx, dz):
        ref, sem = block(part, g, dx, dz)
        arrived(ref, sem)

    def reach(plus, far):
        return (4 if far else 3) if plus else (3 if far else 4)

    def along_z(part, g, dx, s, far):
        if s == 0:
            relay(part, g, dx, 0, 0, 1)
            relay(part, g, dx, 0, 0, -1)
            return
        for plus in (True, False):
            if s <= reach(plus, far):
                dz = -s if plus else s
                come(part, g, dx, dz)
                if s < reach(plus, far):
                    relay(part, g, dx, dz, 0, 1 if plus else -1)

    def steps(part, g, dx, s, far):
        return [(-s if plus else s) for plus in (True, False) if s <= reach(plus, far)]

    def launch(g):
        along_z(1, g, 0, 0, g % 2 == 0)
        for dx in (1, -1, 2):
            relay(0, g, 0, 0, dx, 0)
        relay(1, g, 0, 0, 1, 0)
        relay(1, g, 0, 0, -1, 0)
        along_z(0, g, 0, 0, True)

    def x_hop(g, dz):
        come(1, g, -1, dz)
        if dz % 2 == 0:
            relay(1, g, -1, dz, 1, 0)
        come(1, g, 1, dz)
        if dz % 2 == 1:
            relay(1, g, 1, dz, -1, 0)

    def step(g, s):
        far_b = g % 2 == 0
        if s == 1:
            for dx in (1, -1, 2):
                come(0, g, dx, 0)
                along_z(0, g, dx, 0, dx == 2)
        if s <= 4:
            along_z(1, g, 0, s, far_b)
            for dz in steps(1, g, 0, s, far_b):
                relay(1, g, 0, dz, 1, 0)
                relay(1, g, 0, dz, -1, 0)
        if s >= 2:
            for dx in (0, 1, -1, 2):
                along_z(0, g, dx, s - 1, dx in (0, 2))
        for dz in steps(1, g, 0, s - 1, far_b) if s > 1 else [0]:
            x_hop(g, dz)

    for g in range(GROUPS):
        attend(g)
        launch(g)
    for s in range(1, 6):
        for g in range(GROUPS):
            step(g, s)
    for s in range(5):
        for g in range(GROUPS):
            for dz in steps(1, g, 0, s, g % 2 == 0) if s else [0]:
                come(1, g, 2, dz)

    load_proj.wait()

    def by_target(r):
        j, rest = r // 16, r % 16
        return (rest // 2) * 16 + 2 * j + rest % 2

    for k in (0, 1, 3, 2):
        origin = (ctx + k) % 4
        rows = heads[pl.ds(origin * 8, 8)].reshape(128, 2048)
        product = nn_dot(rows, proj[...]).astype(BF16)
        partial[origin] = permuted(by_target, product).reshape(8, 16, 224)
        sums[origin, tp] = partial[origin, tp]
        for dy in range(4):
            for other in (False, True):
                if dy or other:
                    device = at_tp(dy, other)
                    send(partial.at[origin, device[1]], sums.at[origin, tp], sum_sem.at[origin * 8 + tp], device)
    totals = []
    for origin in range(4):
        for dy in range(4):
            for other in (False, True):
                if dy or other:
                    source = at_tp(dy, other)[1]
                    arrived(sums.at[origin, source], sum_sem.at[origin * 8 + source])
    for origin in range(4):
        total = jnp.zeros((16, 224), F32)
        for source in range(8):
            total = total + sums[origin, source].astype(F32)
        totals.append(total.astype(BF16))

    def by_slot(r):
        return ((r // 2) % 4) * 16 + ((r // 8) % 2) * 8 + (r // 16) * 2 + r % 2

    out_ref[...] = permuted(by_slot, jnp.concatenate(totals, axis=0))
    for copy in started:
        copy.wait_send()


SENDS = 448


def on_device(cache, lengths, slots, parents, nope, rope, latent_rows, key_up, value_up, proj):
    anywhere = pl.BlockSpec(memory_space=pl.ANY)
    in_vmem = pl.BlockSpec(memory_space=pltpu.VMEM)
    in_smem = pl.BlockSpec(memory_space=pltpu.SMEM)
    dma = pltpu.SemaphoreType.DMA
    out = pl.pallas_call(
        kernel,
        out_shape=jax.ShapeDtypeStruct((64, 224), BF16),
        in_specs=[anywhere, in_smem, in_smem, in_vmem] + [anywhere] * 6,
        out_specs=in_vmem,
        scratch_shapes=[
            pltpu.VMEM((8, 32, 576), BF16),
            pltpu.VMEM((8, 8, 128), jnp.int32),
            pltpu.VMEM((32, 32, 640), BF16),
            pltpu.VMEM((8, 2, 16, 128), BF16),
            pltpu.VMEM((8, 2, 16, 64), BF16),
            pltpu.VMEM((64, 576), BF16),
            pltpu.VMEM((16, 128, 512), BF16),
            pltpu.VMEM((16, 512, 128), BF16),
            pltpu.VMEM((2048, 224), BF16),
            pltpu.VMEM((256, 640), BF16),
            pltpu.VMEM((32, 16, 2048), BF16),
            pltpu.VMEM((4, 8, 16, 224), BF16),
            pltpu.VMEM((4, 8, 16, 224), BF16),
            dma((8,)), dma((8,)), dma((8,)), dma((32,)), dma((GROUPS * 32,)), dma((GROUPS * 32,)), dma((32,)),
            dma((SENDS,)),
        ],
        compiler_params=pltpu.CompilerParams(
            collective_id=0, has_side_effects=True, vmem_limit_bytes=48 * 1024 * 1024
        ),
        name="tree_attention",
    )(
        cache.reshape(cache.shape[1:]), lengths, slots, parents,
        nope.reshape(8, 8, 16, 128), rope.reshape(8, 8, 16, 64), latent_rows.reshape(latent_rows.shape[1:]),
        key_up, value_up, proj,
    )
    return out.reshape(8, 8, 224)


def solution(mesh):
    return jax.shard_map(
        on_device,
        mesh=mesh,
        in_specs=(
            P("dec", "ctx", None),
            P("dec"),
            P(),
            P("dec", None),
            P("dec", None, "tp", None),
            P("dec", None, "tp", None),
            P("dec", None, None),
            P("tp", None, None),
            P("tp", None, None),
            P("tp", ("ctx", "dec")),
        ),
        out_specs=P(None, "tp", ("ctx", "dec")),
        check_vma=False,
    )
```

time: 291 us -> 75.5 us (0.26)
  waiting for transfers between devices: 158 us -> 0 us
  Pallas kernels: 0 us -> 66.3 us
  local copies, waits for them, and re-layouts: 38.7 us -> 8.04 us
  blocking collectives: 30.2 us -> 0 us
  starting transfers between devices: 23 us -> 0 us
  between operations: 14.5 us -> 0.85 us
  matrix products: 13.2 us -> 0 us
  other arithmetic: 12 us -> 0 us
    all_gather x1 -> x0, waiting for transfers between devices: 126 us -> none  [on_device(): lax.all_gather(head_values[None], ('ctx', 'dec'), axis=0, tiled=True)]
    pallas_call x0 -> x1, Pallas kernels: none -> 66.3 us  [on_device(): pl.pallas_call(kernel, out_shape=jax.ShapeDtypeStruct((64, 224), BF16), i...]
    all_to_all x4 -> x0, waiting for transfers between devices: 32.1 us -> none  [the longest x1 17.5 us: sent_to_all(): return lax.all_to_all(copies, axis, split_axis=0, concat_axis=0, tiled=True)]
    all_to_all x1 -> x0, blocking collectives: 30.2 us -> none  [sent_and_summed(): blocks = lax.all_to_all(in_blocks(value, dim, size), axis, 0, 0, tiled=True)]
    all_to_all x4 -> x0, starting transfers between devices: 22.9 us -> none  [the longest x3 16.6 us: on_device(): lax.all_to_all(for_sending(stacked), 'ctx', split_axis=2, concat_axis=0,...]
    dot_general x16 -> x0, matrix products: 13.2 us -> none  [the longest x2 3.82 us: to_values(): jnp.einsum('snhc,hcv->snhv', part[2], value_weight, precision=lax.Precisi...]
    unnamed x31 -> x17, local copies, waits for them, and re-layouts: 18.9 us -> 8.04 us
    slice x2 -> x0, local copies, waits for them, and re-layouts: 6.41 us -> none  [sent_together(): piece = whole[..., at:at + column.shape[along]]]
  transfers between devices with their start and end apart: 5 -> 0, of which waited for: 5 -> 0; matrix products, arithmetic and copies ran while one was open for 6% -> 0% of each run, Pallas kernels for 0% -> 0%
where the time goes in v1:
time: 75.5 us; the launch traced here: 75.2 us
  Pallas kernels  66.3 us (88%)
  local copies, waits for them, and re-layouts  8.04 us (11%)
  between operations  0.85 us (1%)
    pallas_call x1, Pallas kernels, on_device(): pl.pallas_call(kernel, out_shape=jax.ShapeDtypeStruct((64, 224), BF16), i...  66.3 us
    unnamed x17, local copies, waits for them, and re-layouts  8.04 us

profile of v1, /device:TPU:1, one launch (start us, length us, event | category | flops | bytes accessed | tf_op | source)
XLA Modules:
  0.0 75.2 jit_solution(10151580515176359795)
XLA Ops:
  0.0 0.0 copy-start
  0.0 0.0 copy-start.4
  0.8 1.2 %copy.11 = bf16[1,256,576]{2,1,0:T(8,128)(2,1)S(1)} copy(bf16[1,256,576]{1,2,0:T(8,128)(2,1)} %param.10) | data formatting | bytes 589824 | tf_op args[0]
  2.0 1.5 %copy.12.proj_ref = bf16[2048,224]{1,0:T(8,128)(2,1)S(1)} copy(bf16[2048,224]{0,1:T(8,128)(2,1)} %param.19) | data formatting | bytes 1835008 | tf_op args[9]
  3.4 0.0 copy-done
  3.4 0.0 copy-done.4
  3.5 0.0 copy-start.1
  3.5 1.6 %copy-done.1 = bf16[16,512,128]{2,1,0:T(8,128)(2,1)S(1)} copy-done((bf16[16,512,128]{2,1,0:T(8,128)(2,1)S(1)}, bf16[16,512,128]{2,1,0:T(8,128)(2,1)}, u32[]{:S(2)}) %copy-start.1) | copy-done | bytes 2097176
  5.0 0.0 copy-start.2
  5.1 0.9 %copy-done.2 = bf16[1,64,16,128]{3,2,1,0:T(8,128)(2,1)S(1)} copy-done((bf16[1,64,16,128]{3,2,1,0:T(8,128)(2,1)S(1)}, bf16[1,64,16,128]{3,2,1,0:T(8,128)(2,1)}, u32[]{:S(2)}) %copy-start.2) | copy-done | bytes 262168
  6.0 0.0 copy-start.3
  6.0 0.9 %copy-done.3 = bf16[1,64,16,64]{3,2,1,0:T(8,128)(2,1)S(1)} copy-done((bf16[1,64,16,64]{3,2,1,0:T(8,128)(2,1)S(1)}, bf16[1,64,16,64]{3,2,1,0:T(8,128)(2,1)}, u32[]{:S(2)}) %copy-start.3) | copy-done | bytes 131096
  7.0 0.0 copy-start.5
  7.0 0.7 copy-done.5
  7.6 0.0 copy-start.6
  7.6 0.7 copy-done.6
  8.3 66.3 %tree_attention.1 = bf16[64,224]{1,0:T(8,128)(2,1)S(1)} custom-call(bf16[256,576]{1,0:T(8,128)(2,1)S(1)} %bitcast.5, s32[1]{0:T(128)S(6)} %copy.14.length_ref, s32[8]{0:T(128)S(1)} %copy-done.5, s32[1,64]{1,0:T(1,128)S(1)} %copy-done.6, bf16[8,8,16,128]{3,2,1,0:T(8,128)(2,1)S(1)} %bitcast.6, bf16[8,8,16,64]{3,2,1,0:T(8,128)(2,1)S(1)} %bitcast.7, ...), custom_call_target="tpu_custom_call" | custom-call | tf_op jit(solution)/shard_map/tree_attention/pallas_call | solution.py:315
  74.6 0.6 copy.15
Async XLA Ops:
  0.0 3.4 %copy-start = (bf16[16,128,512]{2,1,0:T(8,128)(2,1)S(1)}, bf16[16,128,512]{2,1,0:T(8,128)(2,1)}, u32[]{:S(2)}) copy-start(bf16[16,128,512]{2,1,0:T(8,128)(2,1)} %key_up_ref.1) | copy-start | bytes 6291460
  0.0 3.4 %copy-start.4 = (bf16[1,64,576]{2,1,0:T(8,128)(2,1)S(1)}, bf16[1,64,576]{2,1,0:T(8,128)(2,1)}, u32[]{:S(2)}) copy-start(bf16[1,64,576]{2,1,0:T(8,128)(2,1)} %param.16) | copy-start | bytes 221188
  3.5 1.6 %copy-start.1 = (bf16[16,512,128]{2,1,0:T(8,128)(2,1)S(1)}, bf16[16,512,128]{2,1,0:T(8,128)(2,1)}, u32[]{:S(2)}) copy-start(bf16[16,512,128]{2,1,0:T(8,128)(2,1)} %value_up_ref.1) | copy-start | bytes 6291460
  5.0 0.9 %copy-start.2 = (bf16[1,64,16,128]{3,2,1,0:T(8,128)(2,1)S(1)}, bf16[1,64,16,128]{3,2,1,0:T(8,128)(2,1)}, u32[]{:S(2)}) copy-start(bf16[1,64,16,128]{3,2,1,0:T(8,128)(2,1)} %param.14) | copy-start | bytes 786436
  6.0 0.9 %copy-start.3 = (bf16[1,64,16,64]{3,2,1,0:T(8,128)(2,1)S(1)}, bf16[1,64,16,64]{3,2,1,0:T(8,128)(2,1)}, u32[]{:S(2)}) copy-start(bf16[1,64,16,64]{3,2,1,0:T(8,128)(2,1)} %param.15) | copy-start | bytes 393220
  7.0 0.7 copy-start.5
  7.6 0.7 copy-start.6

commit v2 on v1

--- a/solution.py
+++ b/solution.py
@@ -33,7 +33,7 @@
 def kernel(
     cache_ref, length_ref, slot_ref, parents_ref, nope_ref, rope_ref, latent_ref, key_up_ref, value_up_ref, proj_ref,
     out_ref,
-    raw, live, keys, nope, rope, tree_rows, key_up, value_up, proj, queries, heads, partial, sums,
+    raw, live, keys, parents, nope, rope, tree_rows, key_up, value_up, proj, queries, heads, partial, sums,
     local_sem, raw_sem, live_sem, key_sem, a_sem, b_sem, sum_sem, send_sem,
 ):
     ctx, tp, dec = lax.axis_index("ctx"), lax.axis_index("tp"), lax.axis_index("dec")
@@ -87,10 +87,11 @@
         loads.append(copy)
         return copy
 
-    own_rows = cache_ref.at[pl.ds(pl.multiple_of(tp * 32, 32), 32)]
+    own_rows = cache_ref.at[pl.ds(pl.multiple_of(y * 144, 16), 144), pl.ds(pl.multiple_of(core * 128, 128), 128)]
     load_raw = load(own_rows, raw.at[dec])
     load_nope = load(nope_ref.at[:, pl.ds(ctx * 2, 2)], nope)
     load_rope = load(rope_ref.at[:, pl.ds(ctx * 2, 2)], rope)
+    load_parents = load(parents_ref, parents)
     load_tree = load(latent_ref, tree_rows)
     load_key_up = load(key_up_ref, key_up)
     load_value_up = load(value_up_ref, value_up)
@@ -109,7 +110,8 @@
 
     j_at = lax.broadcasted_iota(jnp.int32, (64, 64), 0)
     i_at = lax.broadcasted_iota(jnp.int32, (64, 64), 1)
-    closure = jnp.where((parents_ref[...] == j_at) | (i_at == j_at), 1.0, 0.0)
+    load_parents.wait()
+    closure = jnp.where((parents[...] == j_at) | (i_at == j_at), 1.0, 0.0)
     for _ in range(6):
         closure = jnp.minimum(nn_dot(closure.astype(BF16), closure.astype(BF16)), 1.0)
     row = lax.broadcasted_iota(jnp.int32, (128, 64), 0) % 16
@@ -124,8 +126,7 @@
     load_rope.wait()
     nope_rows = permuted(by_head, nope[...].reshape(256, 128))
     rope_rows = permuted(by_head, rope[...].reshape(256, 64))
-    lane = lax.broadcasted_iota(jnp.int32, (256, 64), 1)
-    queries[:, 512:640] = jnp.concatenate([rope_rows, jnp.where(lane == 0, 1.0, 0.0).astype(BF16)], axis=1)
+    queries[:, 512:576] = rope_rows
     load_key_up.wait()
     for h in range(head_count):
         rows = slice(h * nodes, (h + 1) * nodes)
@@ -137,33 +138,41 @@
         arrived(live.at[source], live_sem.at[source])
         arrived(raw.at[source], raw_sem.at[source])
     wanted = slot_ref[dec]
-    position = ctx * 256 + tp * 32 + lax.broadcasted_iota(jnp.int32, (32, 64), 0)
-    first_lane = lax.broadcasted_iota(jnp.int32, (32, 64), 1) == 0
-    dead = (position >= live[wanted][0:1, 0:64]) & first_lane
-    keys[ctx * 8 + tp] = jnp.concatenate([raw[wanted], jnp.where(dead, DEAD, 0.0).astype(BF16)], axis=1)
-
-    def pass_on(slot, device):
-        send(keys.at[slot], keys.at[slot], key_sem.at[slot], device)
-
-    own_slot = ctx * 8 + tp
+    position = lax.broadcasted_iota(jnp.int32, (8, 128), 1)
+    length = live[wanted]
+    bias = jnp.concatenate(
+        [jnp.where(position + start < length, 0.0, DEAD)[0:1] for start in range(0, 1024, 128)], axis=1
+    )
+
+    def key_part(c, t):
+        rows = pl.ds(pl.multiple_of((t // 2) * 144, 16), 144)
+        return keys.at[rows, pl.ds(pl.multiple_of(c * 256 + (t % 2) * 128, 128), 128)]
+
+    key_part(ctx, tp)[...] = raw[wanted]
+
+    def pass_on(k, t, device):
+        c = (ctx + k) % 4
+        send(key_part(c, t), key_part(c, t), key_sem.at[c * 8 + t], device)
+
+    def come_key(k, t):
+        c = (ctx + k) % 4
+        arrived(key_part(c, t), key_sem.at[c * 8 + t])
+
     for k in (1, 3, 2):
-        pass_on(own_slot, at_ctx(k))
+        pass_on(0, tp, at_ctx(k))
     for k in (0, 1, 3, 2):
-        slot = ((ctx + k) % 4) * 8 + tp
         if k:
-            arrived(keys.at[slot], key_sem.at[slot])
+            come_key(k, tp)
         for dy in (1, 3, 2):
-            pass_on(slot, at_tp(dy))
-        pass_on(slot, at_tp(0, True))
+            pass_on(k, tp, at_tp(dy))
+        pass_on(k, tp, at_tp(0, True))
     for k in (0, 1, 3, 2):
         for dy in (1, 3, 2):
-            slot = ((ctx + k) % 4) * 8 + ((y + dy) % 4) * 2 + core
-            arrived(keys.at[slot], key_sem.at[slot])
-            pass_on(slot, at_tp(0, True))
+            come_key(k, at_tp(dy)[1])
+            pass_on(k, at_tp(dy)[1], at_tp(0, True))
     for k in (0, 1, 3, 2):
         for dy in (0, 1, 3, 2):
-            slot = ((ctx + k) % 4) * 8 + ((y + dy) % 4) * 2 + 1 - core
-            arrived(keys.at[slot], key_sem.at[slot])
+            come_key(k, at_tp(dy, True)[1])
 
     load_tree.wait()
     load_value_up.wait()
@@ -173,13 +182,13 @@
 
     def attend(g):
         q = queries[g * group_rows : (g + 1) * group_rows, :]
-        s = nt_dot(q, keys[...].reshape(1024, 640)) * scale
-        s_tree = nt_dot(q[:, :576], tree_rows[...]) * scale + tree_bias[:group_rows]
+        s = nn_dot(q, keys[...]) * scale + bias
+        s_tree = nt_dot(q, tree_rows[...]) * scale + tree_bias[:group_rows]
         peak = jnp.maximum(jnp.max(s, axis=-1, keepdims=True), jnp.max(s_tree, axis=-1, keepdims=True))
         e = jnp.exp(s - peak)
         e_tree = jnp.exp(s_tree - peak)
         total = jnp.sum(e, axis=-1, keepdims=True) + jnp.sum(e_tree, axis=-1, keepdims=True)
-        o = nn_dot(e.astype(BF16), keys[:, :, 0:512].reshape(1024, 512))
+        o = nt_dot(e.astype(BF16), keys[0:512, :])
         o = o + nn_dot(e_tree.astype(BF16), tree_rows[:, 0:512])
         o = (o / total).astype(BF16)
         for h in range(group_heads):
@@ -275,7 +284,7 @@
     for k in (0, 1, 3, 2):
         origin = (ctx + k) % 4
         rows = heads[pl.ds(origin * 8, 8)].reshape(128, 2048)
-        product = nn_dot(rows, proj[...]).astype(BF16)
+        product = nt_dot(rows, proj[...]).astype(BF16)
         partial[origin] = permuted(by_target, product).reshape(8, 16, 224)
         sums[origin, tp] = partial[origin, tp]
         for dy in range(4):
@@ -315,19 +324,20 @@
     out = pl.pallas_call(
         kernel,
         out_shape=jax.ShapeDtypeStruct((64, 224), BF16),
-        in_specs=[anywhere, in_smem, in_smem, in_vmem] + [anywhere] * 6,
+        in_specs=[anywhere, in_smem, in_smem] + [anywhere] * 7,
         out_specs=in_vmem,
         scratch_shapes=[
-            pltpu.VMEM((8, 32, 576), BF16),
+            pltpu.VMEM((8, 144, 128), BF16),
             pltpu.VMEM((8, 8, 128), jnp.int32),
-            pltpu.VMEM((32, 32, 640), BF16),
+            pltpu.VMEM((576, 1024), BF16),
+            pltpu.VMEM((1, 64), jnp.int32),
             pltpu.VMEM((8, 2, 16, 128), BF16),
             pltpu.VMEM((8, 2, 16, 64), BF16),
             pltpu.VMEM((64, 576), BF16),
             pltpu.VMEM((16, 128, 512), BF16),
             pltpu.VMEM((16, 512, 128), BF16),
-            pltpu.VMEM((2048, 224), BF16),
-            pltpu.VMEM((256, 640), BF16),
+            pltpu.VMEM((224, 2048), BF16),
+            pltpu.VMEM((256, 576), BF16),
             pltpu.VMEM((32, 16, 2048), BF16),
             pltpu.VMEM((4, 8, 16, 224), BF16),
             pltpu.VMEM((4, 8, 16, 224), BF16),
@@ -335,13 +345,13 @@
             dma((SENDS,)),
         ],
         compiler_params=pltpu.CompilerParams(
-            collective_id=0, has_side_effects=True, vmem_limit_bytes=48 * 1024 * 1024
+            collective_id=0, has_side_effects=True, vmem_limit_bytes=58 * 1024 * 1024
         ),
         name="tree_attention",
     )(
-        cache.reshape(cache.shape[1:]), lengths, slots, parents,
+        cache[0].T, lengths, slots, parents,
         nope.reshape(8, 8, 16, 128), rope.reshape(8, 8, 16, 64), latent_rows.reshape(latent_rows.shape[1:]),
-        key_up, value_up, proj,
+        key_up, value_up, proj.T,
     )
     return out.reshape(8, 8, 224)
 

time: 75.5 us -> 69.4 us (0.919)
  local copies, waits for them, and re-layouts: 8.04 us -> 1.38 us
  Pallas kernels: 66.3 us -> 67.2 us
    unnamed x17 -> x1, local copies, waits for them, and re-layouts: 8.04 us -> 1.38 us
    pallas_call x1, Pallas kernels: 66.3 us -> 67.2 us  [on_device(): pl.pallas_call(kernel, out_shape=jax.ShapeDtypeStruct((64, 224), BF16), i...]
where the time goes in v2:
time: 69.4 us; the launch traced here: 69.2 us
  Pallas kernels  67.2 us (97%)
  local copies, waits for them, and re-layouts  1.38 us (2%)
    pallas_call x1, Pallas kernels, on_device(): pl.pallas_call(kernel, out_shape=jax.ShapeDtypeStruct((64, 224), BF16), i...  67.2 us

profile of v2, /device:TPU:1, one launch (start us, length us, event | category | flops | bytes accessed | tf_op | source)
XLA Modules:
  0.0 69.2 jit_solution(16217437609147156389)
XLA Ops:
  0.7 67.2 %tree_attention.1 = bf16[64,224]{1,0:T(8,128)(2,1)} custom-call(bf16[576,256]{1,0:T(8,128)(2,1)} %bitcast.9, s32[1]{0:T(128)S(6)} %copy.12.length_ref, s32[8]{0:T(128)} %slot_ref.1, s32[1,64]{1,0:T(1,128)} %parents_ref.1, bf16[8,8,16,128]{3,2,1,0:T(8,128)(2,1)} %bitcast.10, bf16[8,8,16,64]{3,2,1,0:T(8,128)(2,1)} %bitcast.11, bf16[64,576]{1,0:T(8,128)(2,1)} %bitcast.13, ...), custom_call_target="tpu_custom_call" | custom-call | tf_op jit(solution)/shard_map/tree_attention/pallas_call | solution.py:324
  67.9 1.4 %copy.13 = bf16[8,8,224]{2,1,0:T(8,128)(2,1)} copy(bf16[8,8,224]{2,1,0:T(8,128)(2,1)} %bitcast.12) | data formatting | bytes 57344

commit v3 on v2

--- a/solution.py
+++ b/solution.py
@@ -12,6 +12,10 @@
 BF16 = jnp.bfloat16
 GROUPS = 2
 DEAD = -1e30
+OFFSETS = [0, -1, 1, -2, 2, -3, 3, -4, 4]
+HEAD_SEMS = ["a", "near", "far"]
+HEAD_SEMS += [f"{part}{dz}" for part in ("a", "b") for dz in OFFSETS[1:]]
+HEAD_SEMS += [f"x{side}{dz}" for side in "-+" for dz in OFFSETS]
 
 
 def nt_dot(a, b):
@@ -34,7 +38,7 @@
     cache_ref, length_ref, slot_ref, parents_ref, nope_ref, rope_ref, latent_ref, key_up_ref, value_up_ref, proj_ref,
     out_ref,
     raw, live, keys, parents, nope, rope, tree_rows, key_up, value_up, proj, queries, heads, partial, sums,
-    local_sem, raw_sem, live_sem, key_sem, a_sem, b_sem, sum_sem, send_sem,
+    local_sem, raw_sem, key_sem, head_sem, send_sem,
 ):
     ctx, tp, dec = lax.axis_index("ctx"), lax.axis_index("tp"), lax.axis_index("dec")
     x, z_lo = dec // 2, dec % 2
@@ -63,21 +67,22 @@
     away = (z + 7 + 2 * z_lo) % 8
     peers.append((away // 2, tp, x * 2 + away % 2))
 
-    started = []
-
-    def send(src, dst, sem, device):
-        copy = pltpu.make_async_remote_copy(
-            src_ref=src, dst_ref=dst, send_sem=send_sem.at[len(started)], recv_sem=sem,
+    LIVE, RAW, KEYS, HEADS, SUMS = range(5)
+
+    def described(src, dst, kind, sem, device):
+        return pltpu.make_async_remote_copy(
+            src_ref=src, dst_ref=dst, send_sem=send_sem.at[kind], recv_sem=sem,
             device_id=device, device_id_type=MESH,
         )
-        copy.start()
-        started.append(copy)
+
+    def send(kind, ref, dst, sem, device):
+        described(ref, dst, kind, sem, device).start()
 
     def arrived(dst, sem):
-        pltpu.make_async_remote_copy(
-            src_ref=dst, dst_ref=dst, send_sem=send_sem.at[0], recv_sem=sem,
-            device_id=at_dec(1), device_id_type=MESH,
-        ).wait_recv()
+        described(dst, dst, 0, sem, at_dec(1)).wait_recv()
+
+    def all_sent(kind, as_many_bytes):
+        described(as_many_bytes, as_many_bytes, kind, raw_sem.at[0], at_dec(1)).wait_send()
 
     loads = []
 
@@ -105,8 +110,8 @@
     pl.semaphore_wait(barrier, len(peers))
 
     for k in range(1, 8):
-        send(live.at[dec], live.at[dec], live_sem.at[dec], at_dec(k))
-        send(own_rows, raw.at[dec], raw_sem.at[dec], at_dec(k))
+        send(LIVE, live.at[dec], live.at[dec], raw_sem.at[1], at_dec(k))
+        send(RAW, own_rows, raw.at[dec], raw_sem.at[0], at_dec(k))
 
     j_at = lax.broadcasted_iota(jnp.int32, (64, 64), 0)
     i_at = lax.broadcasted_iota(jnp.int32, (64, 64), 1)
@@ -133,10 +138,8 @@
         queries[rows, 0:512] = nn_dot(nope_rows[rows], key_up[h]).astype(BF16)
 
     load_raw.wait()
-    for k in range(1, 8):
-        source = (dec + k) % 8
-        arrived(live.at[source], live_sem.at[source])
-        arrived(raw.at[source], raw_sem.at[source])
+    arrived(live.at[pl.ds(0, 7)], raw_sem.at[1])
+    arrived(raw.at[pl.ds(0, 7)], raw_sem.at[0])
     wanted = slot_ref[dec]
     position = lax.broadcasted_iota(jnp.int32, (8, 128), 1)
     length = live[wanted]
@@ -150,29 +153,26 @@
 
     key_part(ctx, tp)[...] = raw[wanted]
 
-    def pass_on(k, t, device):
+    def key_piece(k, t, sem, device):
         c = (ctx + k) % 4
-        send(key_part(c, t), key_part(c, t), key_sem.at[c * 8 + t], device)
-
-    def come_key(k, t):
-        c = (ctx + k) % 4
-        arrived(key_part(c, t), key_sem.at[c * 8 + t])
+        send(KEYS, key_part(c, t), key_part(c, t), key_sem.at[sem], device)
+
+    def come_key(k, t, sem):
+        arrived(key_part((ctx + k) % 4, t), key_sem.at[sem])
 
     for k in (1, 3, 2):
-        pass_on(0, tp, at_ctx(k))
+        key_piece(0, tp, (4 - k) * 4, at_ctx(k))
     for k in (0, 1, 3, 2):
         if k:
-            come_key(k, tp)
+            come_key(k, tp, k * 4)
         for dy in (1, 3, 2):
-            pass_on(k, tp, at_tp(dy))
-        pass_on(k, tp, at_tp(0, True))
+            key_piece(k, tp, k * 4 + 4 - dy, at_tp(dy))
+        key_piece(k, tp, 0, at_tp(0, True))
     for k in (0, 1, 3, 2):
         for dy in (1, 3, 2):
-            come_key(k, at_tp(dy)[1])
-            pass_on(k, at_tp(dy)[1], at_tp(0, True))
-    for k in (0, 1, 3, 2):
-        for dy in (0, 1, 3, 2):
-            come_key(k, at_tp(dy, True)[1])
+            come_key(k, at_tp(dy)[1], k * 4 + dy)
+            key_piece(k, at_tp(dy)[1], 0, at_tp(0, True))
+    arrived(keys.at[pl.ds(0, 288)], key_sem.at[0])
 
     load_tree.wait()
     load_value_up.wait()
@@ -199,106 +199,120 @@
     a_width = group_heads * 3 // 8 * 128
     b_width = group_heads * 128 - a_width
 
+    A, B = 0, 1
+
+    def columns(part, g):
+        start = g * group_heads * 128 + (0 if part == A else a_width)
+        return pl.ds(start, a_width if part == A else b_width)
+
     def block(part, g, dx, dz):
-        slot = ((z + dz + 8) % 8) * 4 + (x + dx + 4) % 4
-        start = g * group_heads * 128 + (0 if part == 0 else a_width)
-        ref = heads.at[slot, :, pl.ds(start, a_width if part == 0 else b_width)]
-        return ref, (a_sem, b_sem)[part].at[g * 32 + slot]
-
-    def relay(part, g, dx, dz, to_dx, to_dz):
-        ref, sem = block(part, g, dx, dz)
-        send(ref, ref, sem, at_x(to_dx, to_dz))
-
-    def come(part, g, dx, dz):
-        ref, sem = block(part, g, dx, dz)
-        arrived(ref, sem)
-
-    def reach(plus, far):
-        return (4 if far else 3) if plus else (3 if far else 4)
-
-    def along_z(part, g, dx, s, far):
-        if s == 0:
-            relay(part, g, dx, 0, 0, 1)
-            relay(part, g, dx, 0, 0, -1)
-            return
-        for plus in (True, False):
-            if s <= reach(plus, far):
-                dz = -s if plus else s
-                come(part, g, dx, dz)
-                if s < reach(plus, far):
-                    relay(part, g, dx, dz, 0, 1 if plus else -1)
-
-    def steps(part, g, dx, s, far):
-        return [(-s if plus else s) for plus in (True, False) if s <= reach(plus, far)]
+        return heads.at[((z + dz + 8) % 8) * 4 + (x + dx + 4) % 4, :, columns(part, g)]
+
+    def column_blocks(g, dz, first, count):
+        return heads.at[pl.ds(((z + dz + 8) % 8) * 4 + first, count), :, columns(A, g)]
+
+    def sem_of(g, name):
+        return head_sem.at[g * len(HEAD_SEMS) + HEAD_SEMS.index(name)]
+
+    def go(ref, g, name, dx, dz):
+        send(HEADS, ref, ref, sem_of(g, name), at_x(dx, dz))
+
+    def far_side(part, g):
+        return 1 if (g % 2 == 0) == (part == B) else -1
+
+    def sides(g, s):
+        return (-s, s) if s < 4 else ((-4,) if far_side(B, g) == 1 else (4,))
 
     def launch(g):
-        along_z(1, g, 0, 0, g % 2 == 0)
+        own = block(B, g, 0, 0)
+        go(own, g, "b-1", 0, 1)
+        go(own, g, "b1", 0, -1)
         for dx in (1, -1, 2):
-            relay(0, g, 0, 0, dx, 0)
-        relay(1, g, 0, 0, 1, 0)
-        relay(1, g, 0, 0, -1, 0)
-        along_z(0, g, 0, 0, True)
-
-    def x_hop(g, dz):
-        come(1, g, -1, dz)
-        if dz % 2 == 0:
-            relay(1, g, -1, dz, 1, 0)
-        come(1, g, 1, dz)
-        if dz % 2 == 1:
-            relay(1, g, 1, dz, -1, 0)
-
-    def step(g, s):
-        far_b = g % 2 == 0
-        if s == 1:
-            for dx in (1, -1, 2):
-                come(0, g, dx, 0)
-                along_z(0, g, dx, 0, dx == 2)
-        if s <= 4:
-            along_z(1, g, 0, s, far_b)
-            for dz in steps(1, g, 0, s, far_b):
-                relay(1, g, 0, dz, 1, 0)
-                relay(1, g, 0, dz, -1, 0)
-        if s >= 2:
-            for dx in (0, 1, -1, 2):
-                along_z(0, g, dx, s - 1, dx in (0, 2))
-        for dz in steps(1, g, 0, s - 1, far_b) if s > 1 else [0]:
-            x_hop(g, dz)
-
-    for g in range(GROUPS):
-        attend(g)
-        launch(g)
-    for s in range(1, 6):
-        for g in range(GROUPS):
-            step(g, s)
-    for s in range(5):
-        for g in range(GROUPS):
-            for dz in steps(1, g, 0, s, g % 2 == 0) if s else [0]:
-                come(1, g, 2, dz)
-
-    load_proj.wait()
-
-    def by_target(r):
-        j, rest = r // 16, r % 16
-        return (rest // 2) * 16 + 2 * j + rest % 2
-
-    for k in (0, 1, 3, 2):
+            go(block(A, g, 0, 0), g, "a", dx, 0)
+        go(own, g, "x-0", 1, 0)
+        go(own, g, "x+0", -1, 0)
+
+    def a_launch(g):
+        arrived(heads.at[pl.ds(0, 3), :, columns(A, g)], sem_of(g, "a"))
+        whole = column_blocks(g, 0, 0, 4)
+        go(whole, g, "a-1", 0, 1)
+        go(whole, g, "a1", 0, -1)
+
+    def b_step(g, s):
+        for dz in sides(g, s):
+            ref = block(B, g, 0, dz)
+            arrived(ref, sem_of(g, f"b{dz}"))
+            onward = 1 if dz < 0 else -1
+            if s < 3 or (s == 3 and onward == far_side(B, g)):
+                go(ref, g, f"b{dz - onward}", 0, onward)
+            go(ref, g, f"x-{dz}", 1, 0)
+            go(ref, g, f"x+{dz}", -1, 0)
+
+    def a_step(g, s):
+        if s < 4:
+            for dz in (-s, s):
+                onward = 1 if dz < 0 else -1
+                arrived(column_blocks(g, dz, 0, 4), sem_of(g, f"a{dz}"))
+                if s < 3:
+                    go(column_blocks(g, dz, 0, 4), g, f"a{dz - onward}", 0, onward)
+                else:
+                    go(column_blocks(g, dz, 0 if onward == 1 else 2, 2), g, f"a{dz - onward}", 0, onward)
+        else:
+            for dz in (-4, 4):
+                arrived(column_blocks(g, dz, 0 if dz < 0 else 2, 2), sem_of(g, f"a{dz}"))
+
+    def x_step(g, s):
+        for dz in sides(g, s) if s else (0,):
+            from_left = s == 0 or (dz < 0 if s < 4 else g % 2 == 0)
+            for dx in (-1, 1):
+                ref = block(B, g, dx, dz)
+                arrived(ref, sem_of(g, f"x{'-' if dx < 0 else '+'}{dz}"))
+                if (dx < 0) == from_left:
+                    go(ref, g, "near" if s < 2 else "far", -dx, 0)
+
+    def project(k):
         origin = (ctx + k) % 4
         rows = heads[pl.ds(origin * 8, 8)].reshape(128, 2048)
         product = nt_dot(rows, proj[...]).astype(BF16)
         partial[origin] = permuted(by_target, product).reshape(8, 16, 224)
         sums[origin, tp] = partial[origin, tp]
-        for dy in range(4):
+        for dy in (2, 1, 3, 0):
             for other in (False, True):
                 if dy or other:
                     device = at_tp(dy, other)
-                    send(partial.at[origin, device[1]], sums.at[origin, tp], sum_sem.at[origin * 8 + tp], device)
+                    send(SUMS, partial.at[origin, device[1]], sums.at[origin, tp], raw_sem.at[2], device)
+
+    def by_target(r):
+        j, rest = r // 16, r % 16
+        return (rest // 2) * 16 + 2 * j + rest % 2
+
+    groups = range(GROUPS)
+    for g in groups:
+        attend(g)
+        launch(g)
+    for g in groups:
+        a_launch(g)
+    load_proj.wait()
+    for s in range(1, 6):
+        if s < 5:
+            for g in groups:
+                b_step(g, s)
+        if s > 1:
+            for g in groups:
+                a_step(g, s - 1)
+        for g in groups:
+            x_step(g, s - 1)
+        if s == 4:
+            for g in groups:
+                arrived(heads.at[pl.ds(0, 3), :, columns(B, g)], sem_of(g, "near"))
+            project(0)
+    for g in groups:
+        arrived(heads.at[pl.ds(0, 5), :, columns(B, g)], sem_of(g, "far"))
+    for k in (1, 3, 2):
+        project(k)
+    every = sums.reshape(32, 16, 224)
+    arrived(every.at[pl.ds(0, 28)], raw_sem.at[2])
     totals = []
-    for origin in range(4):
-        for dy in range(4):
-            for other in (False, True):
-                if dy or other:
-                    source = at_tp(dy, other)[1]
-                    arrived(sums.at[origin, source], sum_sem.at[origin * 8 + source])
     for origin in range(4):
         total = jnp.zeros((16, 224), F32)
         for source in range(8):
@@ -309,11 +323,11 @@
         return ((r // 2) % 4) * 16 + ((r // 8) % 2) * 8 + (r // 16) * 2 + r % 2
 
     out_ref[...] = permuted(by_slot, jnp.concatenate(totals, axis=0))
-    for copy in started:
-        copy.wait_send()
-
-
-SENDS = 448
+    all_sent(LIVE, live.at[pl.ds(0, 7)])
+    all_sent(RAW, raw.at[pl.ds(0, 7)])
+    all_sent(KEYS, value_up.reshape(8192, 128).at[pl.ds(0, 31 * 144)])
+    all_sent(HEADS, heads.at[pl.ds(0, 31)])
+    all_sent(SUMS, every.at[pl.ds(0, 28)])
 
 
 def on_device(cache, lengths, slots, parents, nope, rope, latent_rows, key_up, value_up, proj):
@@ -341,8 +355,7 @@
             pltpu.VMEM((32, 16, 2048), BF16),
             pltpu.VMEM((4, 8, 16, 224), BF16),
             pltpu.VMEM((4, 8, 16, 224), BF16),
-            dma((8,)), dma((8,)), dma((8,)), dma((32,)), dma((GROUPS * 32,)), dma((GROUPS * 32,)), dma((32,)),
-            dma((SENDS,)),
+            dma((8,)), dma((3,)), dma((16,)), dma((GROUPS * len(HEAD_SEMS),)), dma((5,)),
         ],
         compiler_params=pltpu.CompilerParams(
             collective_id=0, has_side_effects=True, vmem_limit_bytes=58 * 1024 * 1024

time: 69.4 us -> 65 us (0.937)
  Pallas kernels: 67.2 us -> 62.8 us
    pallas_call x1, Pallas kernels: 67.2 us -> 62.8 us  [on_device(): pl.pallas_call(kernel, out_shape=jax.ShapeDtypeStruct((64, 224), BF16), i...]
where the time goes in v3:
time: 65 us; the launch traced here: 64.9 us
  Pallas kernels  62.8 us (97%)
  local copies, waits for them, and re-layouts  1.38 us (2%)
  between operations  0.66 us (1%)
    pallas_call x1, Pallas kernels, on_device(): pl.pallas_call(kernel, out_shape=jax.ShapeDtypeStruct((64, 224), BF16), i...  62.8 us
    unnamed x1, local copies, waits for them, and re-layouts  1.38 us

profile of v3, /device:TPU:1, one launch (start us, length us, event | category | flops | bytes accessed | tf_op | source)
XLA Modules:
  0.0 64.9 jit_solution(15244752358893768368)
XLA Ops:
  0.7 62.8 %tree_attention.1 = bf16[64,224]{1,0:T(8,128)(2,1)} custom-call(bf16[576,256]{1,0:T(8,128)(2,1)} %bitcast.9, s32[1]{0:T(128)S(6)} %copy.12.length_ref, s32[8]{0:T(128)} %slot_ref.1, s32[1,64]{1,0:T(1,128)} %parents_ref.1, bf16[8,8,16,128]{3,2,1,0:T(8,128)(2,1)} %bitcast.10, bf16[8,8,16,64]{3,2,1,0:T(8,128)(2,1)} %bitcast.11, bf16[64,576]{1,0:T(8,128)(2,1)} %bitcast.13, ...), custom_call_target="tpu_custom_call" | custom-call | tf_op jit(solution)/shard_map/tree_attention/pallas_call | solution.py:338
  63.5 1.4 %copy.13 = bf16[8,8,224]{2,1,0:T(8,128)(2,1)} copy(bf16[8,8,224]{2,1,0:T(8,128)(2,1)} %bitcast.12) | data formatting | bytes 57344

commit v4 on v3

--- a/solution.py
+++ b/solution.py
@@ -13,9 +13,22 @@
 GROUPS = 2
 DEAD = -1e30
 OFFSETS = [0, -1, 1, -2, 2, -3, 3, -4, 4]
-HEAD_SEMS = ["a", "near", "far"]
+HEAD_SEMS = ["a", "near", "mid", "far"]
 HEAD_SEMS += [f"{part}{dz}" for part in ("a", "b") for dz in OFFSETS[1:]]
 HEAD_SEMS += [f"x{side}{dz}" for side in "-+" for dz in OFFSETS]
+
+ORDER = [
+    ("L", 0), ("L", 1), ("b", 0, -1), ("b", 0, 1), ("x", 0, -1, 0), ("a", 0), ("x", 0, 1, 0), ("b", 1, -1),
+    ("b", 1, 1), ("x", 1, 1, 0), ("a", 1), ("x", 1, -1, 0), ("b", 0, -2), ("x", 0, 1, -1), ("b", 0, 2),
+    ("x", 0, -1, -1), ("x", 0, 1, 1), ("x", 0, -1, 1), ("A", 0, -1), ("A", 0, 1), ("x", 1, -1, -1), ("x", 1, 1, -1),
+    ("b", 1, -2), ("b", 1, 2), ("x", 1, -1, 1), ("x", 1, 1, 1), ("x", 0, -1, -2), ("A", 1, -1), ("A", 1, 1),
+    ("x", 0, 1, -2), ("x", 0, -1, 2), ("b", 0, -3), ("b", 0, 3), ("x", 0, 1, 2), ("b", 0, -4), ("x", 1, 1, -2),
+    ("A", 0, 2), ("x", 1, -1, -2), ("x", 1, 1, 2), ("b", 1, 3), ("x", 1, -1, 2), ("A", 0, -2), ("b", 1, -3),
+    ("x", 0, 1, -3), ("x", 0, -1, -3), ("b", 1, 4), ("x", 0, 1, 3), ("x", 0, -1, 3), ("A", 1, -2), ("x", 0, -1, -4),
+    ("A", 1, 2), ("x", 0, 1, -4), ("P", 0), ("x", 1, -1, 3), ("A", 0, 3), ("x", 1, 1, 3), ("x", 1, -1, -3), ("A", 0, -3),
+    ("x", 1, 1, -3), ("x", 1, 1, 4), ("x", 1, -1, 4), ("A", 0, 4), ("A", 0, -4), ("A", 1, 3), ("A", 1, -3), ("P", 1),
+    ("A", 1, 4), ("A", 1, -4),
+]
 
 
 def nt_dot(a, b):
@@ -162,16 +175,25 @@
 
     for k in (1, 3, 2):
         key_piece(0, tp, (4 - k) * 4, at_ctx(k))
-    for k in (0, 1, 3, 2):
+    def along_y(k):
         if k:
             come_key(k, tp, k * 4)
         for dy in (1, 3, 2):
             key_piece(k, tp, k * 4 + 4 - dy, at_tp(dy))
         key_piece(k, tp, 0, at_tp(0, True))
-    for k in (0, 1, 3, 2):
+
+    def to_other_core(k):
         for dy in (1, 3, 2):
             come_key(k, at_tp(dy)[1], k * 4 + dy)
             key_piece(k, at_tp(dy)[1], 0, at_tp(0, True))
+
+    along_y(0)
+    along_y(1)
+    along_y(3)
+    to_other_core(0)
+    along_y(2)
+    for k in (1, 3, 2):
+        to_other_core(k)
     arrived(keys.at[pl.ds(0, 288)], key_sem.at[0])
 
     load_tree.wait()
@@ -220,9 +242,6 @@
     def far_side(part, g):
         return 1 if (g % 2 == 0) == (part == B) else -1
 
-    def sides(g, s):
-        return (-s, s) if s < 4 else ((-4,) if far_side(B, g) == 1 else (4,))
-
     def launch(g):
         own = block(B, g, 0, 0)
         go(own, g, "b-1", 0, 1)
@@ -238,37 +257,36 @@
         go(whole, g, "a-1", 0, 1)
         go(whole, g, "a1", 0, -1)
 
-    def b_step(g, s):
-        for dz in sides(g, s):
-            ref = block(B, g, 0, dz)
-            arrived(ref, sem_of(g, f"b{dz}"))
-            onward = 1 if dz < 0 else -1
-            if s < 3 or (s == 3 and onward == far_side(B, g)):
-                go(ref, g, f"b{dz - onward}", 0, onward)
-            go(ref, g, f"x-{dz}", 1, 0)
-            go(ref, g, f"x+{dz}", -1, 0)
-
-    def a_step(g, s):
-        if s < 4:
-            for dz in (-s, s):
-                onward = 1 if dz < 0 else -1
-                arrived(column_blocks(g, dz, 0, 4), sem_of(g, f"a{dz}"))
-                if s < 3:
-                    go(column_blocks(g, dz, 0, 4), g, f"a{dz - onward}", 0, onward)
-                else:
-                    go(column_blocks(g, dz, 0 if onward == 1 else 2, 2), g, f"a{dz - onward}", 0, onward)
-        else:
-            for dz in (-4, 4):
-                arrived(column_blocks(g, dz, 0 if dz < 0 else 2, 2), sem_of(g, f"a{dz}"))
-
-    def x_step(g, s):
-        for dz in sides(g, s) if s else (0,):
-            from_left = s == 0 or (dz < 0 if s < 4 else g % 2 == 0)
-            for dx in (-1, 1):
-                ref = block(B, g, dx, dz)
-                arrived(ref, sem_of(g, f"x{'-' if dx < 0 else '+'}{dz}"))
-                if (dx < 0) == from_left:
-                    go(ref, g, "near" if s < 2 else "far", -dx, 0)
+    def b_step(g, dz):
+        ref = block(B, g, 0, dz)
+        arrived(ref, sem_of(g, f"b{dz}"))
+        onward = 1 if dz < 0 else -1
+        if abs(dz) <= 2:
+            go(ref, g, f"b{dz - onward}", 0, onward)
+        if abs(dz) == 2 and onward == far_side(B, g):
+            go(ref, g, f"b{dz - 2 * onward}", 0, 2 * onward)
+        go(ref, g, f"x-{dz}", 1, 0)
+        go(ref, g, f"x+{dz}", -1, 0)
+
+    def a_step(g, dz):
+        onward = 1 if dz < 0 else -1
+        half = 0 if onward == 1 else 2
+        if abs(dz) == 4:
+            arrived(column_blocks(g, dz, half, 2), sem_of(g, f"a{dz}"))
+            return
+        whole = column_blocks(g, dz, 0, 4)
+        arrived(whole, sem_of(g, f"a{dz}"))
+        if abs(dz) <= 2:
+            go(whole, g, f"a{dz - onward}", 0, onward)
+        if abs(dz) == 2:
+            go(column_blocks(g, dz, half, 2), g, f"a{dz - 2 * onward}", 0, 2 * onward)
+
+    def x_step(g, dx, dz):
+        ref = block(B, g, dx, dz)
+        arrived(ref, sem_of(g, f"x{'-' if dx < 0 else '+'}{dz}"))
+        from_left = g % 2 == 0 if dz in (0, -4, 4) else dz < 0
+        if (dx < 0) == from_left:
+            go(ref, g, "near" if abs(dz) < 2 else "mid" if abs(dz) < 4 else "far", -dx, 0)
 
     def project(k):
         origin = (ctx + k) % 4
@@ -286,30 +304,27 @@
         j, rest = r // 16, r % 16
         return (rest // 2) * 16 + 2 * j + rest % 2
 
-    groups = range(GROUPS)
-    for g in groups:
-        attend(g)
-        launch(g)
-    for g in groups:
-        a_launch(g)
+    def opposite(name, count):
+        for g in range(GROUPS):
+            arrived(heads.at[pl.ds(0, count), :, columns(B, g)], sem_of(g, name))
+
     load_proj.wait()
-    for s in range(1, 6):
-        if s < 5:
-            for g in groups:
-                b_step(g, s)
-        if s > 1:
-            for g in groups:
-                a_step(g, s - 1)
-        for g in groups:
-            x_step(g, s - 1)
-        if s == 4:
-            for g in groups:
-                arrived(heads.at[pl.ds(0, 3), :, columns(B, g)], sem_of(g, "near"))
-            project(0)
-    for g in groups:
-        arrived(heads.at[pl.ds(0, 5), :, columns(B, g)], sem_of(g, "far"))
-    for k in (1, 3, 2):
-        project(k)
+    for what, *which in ORDER:
+        if what == "L":
+            attend(*which)
+            launch(*which)
+        elif what == "P":
+            if which[0] == 0:
+                opposite("near", 3)
+                project(0)
+            else:
+                opposite("mid", 4)
+                project(1)
+                project(3)
+        else:
+            {"a": a_launch, "A": a_step, "b": b_step, "x": x_step}[what](*which)
+    opposite("far", 1)
+    project(2)
     every = sums.reshape(32, 16, 224)
     arrived(every.at[pl.ds(0, 28)], raw_sem.at[2])
     totals = []

time: 65 us -> 58.8 us (0.905)
  Pallas kernels: 62.8 us -> 56.6 us
    pallas_call x1, Pallas kernels: 62.8 us -> 56.6 us  [on_device(): pl.pallas_call(kernel, out_shape=jax.ShapeDtypeStruct((64, 224), BF16), i...]
where the time goes in v4:
time: 58.8 us; the launch traced here: 58.6 us
  Pallas kernels  56.6 us (96%)
  local copies, waits for them, and re-layouts  1.38 us (2%)
  between operations  0.66 us (1%)
    pallas_call x1, Pallas kernels, on_device(): pl.pallas_call(kernel, out_shape=jax.ShapeDtypeStruct((64, 224), BF16), i...  56.6 us
    unnamed x1, local copies, waits for them, and re-layouts  1.38 us

profile of v4, /device:TPU:1, one launch (start us, length us, event | category | flops | bytes accessed | tf_op | source)
XLA Modules:
  0.0 58.6 jit_solution(3296552522569577366)
XLA Ops:
  0.7 56.6 %tree_attention.1 = bf16[64,224]{1,0:T(8,128)(2,1)} custom-call(bf16[576,256]{1,0:T(8,128)(2,1)} %bitcast.9, s32[1]{0:T(128)S(6)} %copy.12.length_ref, s32[8]{0:T(128)} %slot_ref.1, s32[1,64]{1,0:T(1,128)} %parents_ref.1, bf16[8,8,16,128]{3,2,1,0:T(8,128)(2,1)} %bitcast.10, bf16[8,8,16,64]{3,2,1,0:T(8,128)(2,1)} %bitcast.11, bf16[64,576]{1,0:T(8,128)(2,1)} %bitcast.13, ...), custom_call_target="tpu_custom_call" | custom-call | tf_op jit(solution)/shard_map/tree_attention/pallas_call | solution.py:353
  57.2 1.4 %copy.13 = bf16[8,8,224]{2,1,0:T(8,128)(2,1)} copy(bf16[8,8,224]{2,1,0:T(8,128)(2,1)} %bitcast.12) | data formatting | bytes 57344

commit v5 on v4

--- a/solution.py
+++ b/solution.py
@@ -48,9 +48,9 @@
 
 
 def kernel(
-    cache_ref, length_ref, slot_ref, parents_ref, nope_ref, rope_ref, latent_ref, key_up_ref, value_up_ref, proj_ref,
+    cache_ref, length_ref, slots_ref, parents_ref, nope_ref, rope_ref, latent_ref, key_up_ref, value_up_ref, proj_ref,
     out_ref,
-    raw, live, keys, parents, nope, rope, tree_rows, key_up, value_up, proj, queries, heads, partial, sums,
+    slot_ref, raw, live, keys, parents, nope, rope, tree_rows, key_up, value_up, proj, proj_t, queries, heads, partial, sums,
     local_sem, raw_sem, key_sem, head_sem, send_sem,
 ):
     ctx, tp, dec = lax.axis_index("ctx"), lax.axis_index("tp"), lax.axis_index("dec")
@@ -106,6 +106,7 @@
         return copy
 
     own_rows = cache_ref.at[pl.ds(pl.multiple_of(y * 144, 16), 144), pl.ds(pl.multiple_of(core * 128, 128), 128)]
+    load_slot = load(slots_ref, slot_ref)
     load_raw = load(own_rows, raw.at[dec])
     load_nope = load(nope_ref.at[:, pl.ds(ctx * 2, 2)], nope)
     load_rope = load(rope_ref.at[:, pl.ds(ctx * 2, 2)], rope)
@@ -115,11 +116,10 @@
     load_value_up = load(value_up_ref, value_up)
     load_proj = load(proj_ref, proj)
 
-    live[dec] = jnp.full((8, 128), length_ref[0], jnp.int32)
-
     barrier = pltpu.get_barrier_semaphore()
     for peer in peers:
         pl.semaphore_signal(barrier, inc=1, device_id=peer, device_id_type=MESH)
+    live[dec] = jnp.full((8, 128), length_ref[0], jnp.int32)
     pl.semaphore_wait(barrier, len(peers))
 
     for k in range(1, 8):
@@ -150,9 +150,13 @@
         rows = slice(h * nodes, (h + 1) * nodes)
         queries[rows, 0:512] = nn_dot(nope_rows[rows], key_up[h]).astype(BF16)
 
+    load_proj.wait()
+    proj_t[...] = proj[...].T
+
     load_raw.wait()
     arrived(live.at[pl.ds(0, 7)], raw_sem.at[1])
     arrived(raw.at[pl.ds(0, 7)], raw_sem.at[0])
+    load_slot.wait()
     wanted = slot_ref[dec]
     position = lax.broadcasted_iota(jnp.int32, (8, 128), 1)
     length = live[wanted]
@@ -291,7 +295,7 @@
     def project(k):
         origin = (ctx + k) % 4
         rows = heads[pl.ds(origin * 8, 8)].reshape(128, 2048)
-        product = nt_dot(rows, proj[...]).astype(BF16)
+        product = nn_dot(rows, proj_t[...]).astype(BF16)
         partial[origin] = permuted(by_target, product).reshape(8, 16, 224)
         sums[origin, tp] = partial[origin, tp]
         for dy in (2, 1, 3, 0):
@@ -308,7 +312,6 @@
         for g in range(GROUPS):
             arrived(heads.at[pl.ds(0, count), :, columns(B, g)], sem_of(g, name))
 
-    load_proj.wait()
     for what, *which in ORDER:
         if what == "L":
             attend(*which)
@@ -348,14 +351,14 @@
 def on_device(cache, lengths, slots, parents, nope, rope, latent_rows, key_up, value_up, proj):
     anywhere = pl.BlockSpec(memory_space=pl.ANY)
     in_vmem = pl.BlockSpec(memory_space=pltpu.VMEM)
-    in_smem = pl.BlockSpec(memory_space=pltpu.SMEM)
     dma = pltpu.SemaphoreType.DMA
     out = pl.pallas_call(
         kernel,
         out_shape=jax.ShapeDtypeStruct((64, 224), BF16),
-        in_specs=[anywhere, in_smem, in_smem] + [anywhere] * 7,
+        in_specs=[anywhere, pl.BlockSpec(memory_space=pltpu.SMEM)] + [anywhere] * 8,
         out_specs=in_vmem,
         scratch_shapes=[
+            pltpu.SMEM((8,), jnp.int32),
             pltpu.VMEM((8, 144, 128), BF16),
             pltpu.VMEM((8, 8, 128), jnp.int32),
             pltpu.VMEM((576, 1024), BF16),
@@ -366,11 +369,12 @@
             pltpu.VMEM((16, 128, 512), BF16),
             pltpu.VMEM((16, 512, 128), BF16),
             pltpu.VMEM((224, 2048), BF16),
+            pltpu.VMEM((2048, 224), BF16),
             pltpu.VMEM((256, 576), BF16),
             pltpu.VMEM((32, 16, 2048), BF16),
             pltpu.VMEM((4, 8, 16, 224), BF16),
             pltpu.VMEM((4, 8, 16, 224), BF16),
-            dma((8,)), dma((3,)), dma((16,)), dma((GROUPS * len(HEAD_SEMS),)), dma((5,)),
+            dma((9,)), dma((3,)), dma((16,)), dma((GROUPS * len(HEAD_SEMS),)), dma((5,)),
         ],
         compiler_params=pltpu.CompilerParams(
             collective_id=0, has_side_effects=True, vmem_limit_bytes=58 * 1024 * 1024

time: 58.8 us -> 57.3 us (0.974)
  Pallas kernels: 56.6 us -> 55.1 us
    pallas_call x1, Pallas kernels: 56.6 us -> 55.1 us  [on_device(): pl.pallas_call(kernel, out_shape=jax.ShapeDtypeStruct((64, 224), BF16), i...]
where the time goes in v5:
time: 57.3 us; the launch traced here: 57.2 us
  Pallas kernels  55.1 us (96%)
  local copies, waits for them, and re-layouts  1.38 us (2%)
  between operations  0.66 us (1%)
    pallas_call x1, Pallas kernels, on_device(): pl.pallas_call(kernel, out_shape=jax.ShapeDtypeStruct((64, 224), BF16), i...  55.1 us
    unnamed x1, local copies, waits for them, and re-layouts  1.38 us

profile of v5, /device:TPU:1, one launch (start us, length us, event | category | flops | bytes accessed | tf_op | source)
XLA Modules:
  0.0 57.2 jit_solution(13457849513122116741)
XLA Ops:
  0.7 55.1 %tree_attention.1 = bf16[64,224]{1,0:T(8,128)(2,1)} custom-call(bf16[576,256]{1,0:T(8,128)(2,1)} %bitcast.9, s32[1]{0:T(128)S(6)} %copy.12.length_ref, s32[8]{0:T(128)} %slots_ref.1, s32[1,64]{1,0:T(1,128)} %parents_ref.1, bf16[8,8,16,128]{3,2,1,0:T(8,128)(2,1)} %bitcast.10, bf16[8,8,16,64]{3,2,1,0:T(8,128)(2,1)} %bitcast.11, bf16[64,576]{1,0:T(8,128)(2,1)} %bitcast.13, ...), custom_call_target="tpu_custom_call" | custom-call | tf_op jit(solution)/shard_map/tree_attention/pallas_call | solution.py:355
  55.8 1.4 %copy.13 = bf16[8,8,224]{2,1,0:T(8,128)(2,1)} copy(bf16[8,8,224]{2,1,0:T(8,128)(2,1)} %bitcast.12) | data formatting | bytes 57344

commit v6 on v5

--- a/solution.py
+++ b/solution.py
@@ -15,19 +15,16 @@
 OFFSETS = [0, -1, 1, -2, 2, -3, 3, -4, 4]
 HEAD_SEMS = ["a", "near", "mid", "far"]
 HEAD_SEMS += [f"{part}{dz}" for part in ("a", "b") for dz in OFFSETS[1:]]
-HEAD_SEMS += [f"x{side}{dz}" for side in "-+" for dz in OFFSETS]
+HEAD_SEMS += [f"x{dz}" for dz in OFFSETS]
 
 ORDER = [
-    ("L", 0), ("L", 1), ("b", 0, -1), ("b", 0, 1), ("x", 0, -1, 0), ("a", 0), ("x", 0, 1, 0), ("b", 1, -1),
-    ("b", 1, 1), ("x", 1, 1, 0), ("a", 1), ("x", 1, -1, 0), ("b", 0, -2), ("x", 0, 1, -1), ("b", 0, 2),
-    ("x", 0, -1, -1), ("x", 0, 1, 1), ("x", 0, -1, 1), ("A", 0, -1), ("A", 0, 1), ("x", 1, -1, -1), ("x", 1, 1, -1),
-    ("b", 1, -2), ("b", 1, 2), ("x", 1, -1, 1), ("x", 1, 1, 1), ("x", 0, -1, -2), ("A", 1, -1), ("A", 1, 1),
-    ("x", 0, 1, -2), ("x", 0, -1, 2), ("b", 0, -3), ("b", 0, 3), ("x", 0, 1, 2), ("b", 0, -4), ("x", 1, 1, -2),
-    ("A", 0, 2), ("x", 1, -1, -2), ("x", 1, 1, 2), ("b", 1, 3), ("x", 1, -1, 2), ("A", 0, -2), ("b", 1, -3),
-    ("x", 0, 1, -3), ("x", 0, -1, -3), ("b", 1, 4), ("x", 0, 1, 3), ("x", 0, -1, 3), ("A", 1, -2), ("x", 0, -1, -4),
-    ("A", 1, 2), ("x", 0, 1, -4), ("P", 0), ("x", 1, -1, 3), ("A", 0, 3), ("x", 1, 1, 3), ("x", 1, -1, -3), ("A", 0, -3),
-    ("x", 1, 1, -3), ("x", 1, 1, 4), ("x", 1, -1, 4), ("A", 0, 4), ("A", 0, -4), ("A", 1, 3), ("A", 1, -3), ("P", 1),
-    ("A", 1, 4), ("A", 1, -4),
+    ("L", 0), ("L", 1), ("b", 0, -1), ("b", 0, 1), ("x", 0, 0), ("a", 0), ("b", 1, -1), ("b", 1, 1), ("x", 1, 0),
+    ("a", 1), ("b", 0, -2), ("b", 0, 2), ("x", 0, -1), ("x", 0, 1), ("A", 0, -1), ("A", 0, 1), ("x", 1, -1),
+    ("b", 1, -2), ("b", 1, 2), ("x", 1, 1), ("x", 0, -2), ("A", 1, -1), ("A", 1, 1), ("b", 0, -3), ("b", 0, 3),
+    ("x", 0, 2), ("b", 0, -4), ("A", 0, 2), ("x", 1, -2), ("x", 1, 2), ("b", 1, 3), ("A", 0, -2), ("b", 1, -3),
+    ("x", 0, -3), ("b", 1, 4), ("x", 0, 3), ("A", 1, -2), ("x", 0, -4), ("A", 1, 2), ("P", 0), ("A", 0, 3),
+    ("x", 1, 3), ("x", 1, -3), ("A", 0, -3), ("x", 1, 4), ("A", 0, 4), ("A", 0, -4), ("A", 1, 3), ("A", 1, -3),
+    ("P", 1), ("A", 1, 4), ("A", 1, -4),
 ]
 
 
@@ -122,9 +119,11 @@
     live[dec] = jnp.full((8, 128), length_ref[0], jnp.int32)
     pl.semaphore_wait(barrier, len(peers))
 
+    load_raw.wait()
+    for k in range(1, 8):
+        send(RAW, raw.at[dec], raw.at[dec], raw_sem.at[0], at_dec(k))
     for k in range(1, 8):
         send(LIVE, live.at[dec], live.at[dec], raw_sem.at[1], at_dec(k))
-        send(RAW, own_rows, raw.at[dec], raw_sem.at[0], at_dec(k))
 
     j_at = lax.broadcasted_iota(jnp.int32, (64, 64), 0)
     i_at = lax.broadcasted_iota(jnp.int32, (64, 64), 1)
@@ -145,25 +144,10 @@
     nope_rows = permuted(by_head, nope[...].reshape(256, 128))
     rope_rows = permuted(by_head, rope[...].reshape(256, 64))
     queries[:, 512:576] = rope_rows
-    load_key_up.wait()
-    for h in range(head_count):
-        rows = slice(h * nodes, (h + 1) * nodes)
-        queries[rows, 0:512] = nn_dot(nope_rows[rows], key_up[h]).astype(BF16)
-
-    load_proj.wait()
-    proj_t[...] = proj[...].T
-
-    load_raw.wait()
-    arrived(live.at[pl.ds(0, 7)], raw_sem.at[1])
+
     arrived(raw.at[pl.ds(0, 7)], raw_sem.at[0])
     load_slot.wait()
     wanted = slot_ref[dec]
-    position = lax.broadcasted_iota(jnp.int32, (8, 128), 1)
-    length = live[wanted]
-    bias = jnp.concatenate(
-        [jnp.where(position + start < length, 0.0, DEAD)[0:1] for start in range(0, 1024, 128)], axis=1
-    )
-
     def key_part(c, t):
         rows = pl.ds(pl.multiple_of((t // 2) * 144, 16), 144)
         return keys.at[rows, pl.ds(pl.multiple_of(c * 256 + (t % 2) * 128, 128), 128)]
@@ -192,10 +176,22 @@
             key_piece(k, at_tp(dy)[1], 0, at_tp(0, True))
 
     along_y(0)
+    load_key_up.wait()
+    for h in range(head_count):
+        rows = slice(h * nodes, (h + 1) * nodes)
+        queries[rows, 0:512] = nn_dot(nope_rows[rows], key_up[h]).astype(BF16)
     along_y(1)
     along_y(3)
     to_other_core(0)
     along_y(2)
+    load_proj.wait()
+    proj_t[...] = proj[...].T
+    arrived(live.at[pl.ds(0, 7)], raw_sem.at[1])
+    position = lax.broadcasted_iota(jnp.int32, (8, 128), 1)
+    length = live[wanted]
+    bias = jnp.concatenate(
+        [jnp.where(position + start < length, 0.0, DEAD)[0:1] for start in range(0, 1024, 128)], axis=1
+    )
     for k in (1, 3, 2):
         to_other_core(k)
     arrived(keys.at[pl.ds(0, 288)], key_sem.at[0])
@@ -246,14 +242,24 @@
     def far_side(part, g):
         return 1 if (g % 2 == 0) == (part == B) else -1
 
+    def from_left(g, dz):
+        return g % 2 == 0 if dz in (0, -4, 4) else dz < 0
+
+    def distance(dz):
+        return "near" if abs(dz) < 2 else "mid" if abs(dz) < 4 else "far"
+
+    def to_x(g, dz):
+        ref = block(B, g, 0, dz)
+        go(ref, g, f"x{dz}" if from_left(g, dz) else distance(dz), 1, 0)
+        go(ref, g, distance(dz) if from_left(g, dz) else f"x{dz}", -1, 0)
+
     def launch(g):
         own = block(B, g, 0, 0)
         go(own, g, "b-1", 0, 1)
         go(own, g, "b1", 0, -1)
         for dx in (1, -1, 2):
             go(block(A, g, 0, 0), g, "a", dx, 0)
-        go(own, g, "x-0", 1, 0)
-        go(own, g, "x+0", -1, 0)
+        to_x(g, 0)
 
     def a_launch(g):
         arrived(heads.at[pl.ds(0, 3), :, columns(A, g)], sem_of(g, "a"))
@@ -269,8 +275,7 @@
             go(ref, g, f"b{dz - onward}", 0, onward)
         if abs(dz) == 2 and onward == far_side(B, g):
             go(ref, g, f"b{dz - 2 * onward}", 0, 2 * onward)
-        go(ref, g, f"x-{dz}", 1, 0)
-        go(ref, g, f"x+{dz}", -1, 0)
+        to_x(g, dz)
 
     def a_step(g, dz):
         onward = 1 if dz < 0 else -1
@@ -285,12 +290,11 @@
         if abs(dz) == 2:
             go(column_blocks(g, dz, half, 2), g, f"a{dz - 2 * onward}", 0, 2 * onward)
 
-    def x_step(g, dx, dz):
+    def x_step(g, dz):
+        dx = -1 if from_left(g, dz) else 1
         ref = block(B, g, dx, dz)
-        arrived(ref, sem_of(g, f"x{'-' if dx < 0 else '+'}{dz}"))
-        from_left = g % 2 == 0 if dz in (0, -4, 4) else dz < 0
-        if (dx < 0) == from_left:
-            go(ref, g, "near" if abs(dz) < 2 else "mid" if abs(dz) < 4 else "far", -dx, 0)
+        arrived(ref, sem_of(g, f"x{dz}"))
+        go(ref, g, distance(dz), -dx, 0)
 
     def project(k):
         origin = (ctx + k) % 4
@@ -318,15 +322,15 @@
             launch(*which)
         elif what == "P":
             if which[0] == 0:
-                opposite("near", 3)
+                opposite("near", 6)
                 project(0)
             else:
-                opposite("mid", 4)
+                opposite("mid", 8)
                 project(1)
                 project(3)
         else:
             {"a": a_launch, "A": a_step, "b": b_step, "x": x_step}[what](*which)
-    opposite("far", 1)
+    opposite("far", 2)
     project(2)
     every = sums.reshape(32, 16, 224)
     arrived(every.at[pl.ds(0, 28)], raw_sem.at[2])

time: 57.3 us -> 55.8 us (0.974)
  Pallas kernels: 55.1 us -> 53.6 us
    pallas_call x1, Pallas kernels: 55.1 us -> 53.6 us  [on_device(): pl.pallas_call(kernel, out_shape=jax.ShapeDtypeStruct((64, 224), BF16), i...]
where the time goes in v6:
time: 55.8 us; the launch traced here: 55.6 us
  Pallas kernels  53.6 us (96%)
  local copies, waits for them, and re-layouts  1.38 us (2%)
  between operations  0.66 us (1%)
    pallas_call x1, Pallas kernels, on_device(): pl.pallas_call(kernel, out_shape=jax.ShapeDtypeStruct((64, 224), BF16), i...  53.6 us
    unnamed x1, local copies, waits for them, and re-layouts  1.38 us

profile of v6, /device:TPU:1, one launch (start us, length us, event | category | flops | bytes accessed | tf_op | source)
XLA Modules:
  0.0 55.6 jit_solution(13706516713120176389)
XLA Ops:
  0.7 53.6 %tree_attention.1 = bf16[64,224]{1,0:T(8,128)(2,1)} custom-call(bf16[576,256]{1,0:T(8,128)(2,1)} %bitcast.9, s32[1]{0:T(128)S(6)} %copy.12.length_ref, s32[8]{0:T(128)} %slots_ref.1, s32[1,64]{1,0:T(1,128)} %parents_ref.1, bf16[8,8,16,128]{3,2,1,0:T(8,128)(2,1)} %bitcast.10, bf16[8,8,16,64]{3,2,1,0:T(8,128)(2,1)} %bitcast.11, bf16[64,576]{1,0:T(8,128)(2,1)} %bitcast.13, ...), custom_call_target="tpu_custom_call" | custom-call | tf_op jit(solution)/shard_map/tree_attention/pallas_call | solution.py:359
  54.2 1.4 %copy.13 = bf16[8,8,224]{2,1,0:T(8,128)(2,1)} copy(bf16[8,8,224]{2,1,0:T(8,128)(2,1)} %bitcast.12) | data formatting | bytes 57344

commit v7 on v6

--- a/solution.py
+++ b/solution.py
@@ -10,7 +10,9 @@
 MESH = pl.DeviceIdType.MESH
 F32 = jnp.float32
 BF16 = jnp.bfloat16
-GROUPS = 2
+GROUP_HEADS = (8, 8)
+A_HEADS = (3, 3)
+GROUPS = len(GROUP_HEADS)
 DEAD = -1e30
 OFFSETS = [0, -1, 1, -2, 2, -3, 3, -4, 4]
 HEAD_SEMS = ["a", "near", "mid", "far"]
@@ -18,13 +20,13 @@
 HEAD_SEMS += [f"x{dz}" for dz in OFFSETS]
 
 ORDER = [
-    ("L", 0), ("L", 1), ("b", 0, -1), ("b", 0, 1), ("x", 0, 0), ("a", 0), ("b", 1, -1), ("b", 1, 1), ("x", 1, 0),
-    ("a", 1), ("b", 0, -2), ("b", 0, 2), ("x", 0, -1), ("x", 0, 1), ("A", 0, -1), ("A", 0, 1), ("x", 1, -1),
-    ("b", 1, -2), ("b", 1, 2), ("x", 1, 1), ("x", 0, -2), ("A", 1, -1), ("A", 1, 1), ("b", 0, -3), ("b", 0, 3),
-    ("x", 0, 2), ("b", 0, -4), ("A", 0, 2), ("x", 1, -2), ("x", 1, 2), ("b", 1, 3), ("A", 0, -2), ("b", 1, -3),
-    ("x", 0, -3), ("b", 1, 4), ("x", 0, 3), ("A", 1, -2), ("x", 0, -4), ("A", 1, 2), ("P", 0), ("A", 0, 3),
-    ("x", 1, 3), ("x", 1, -3), ("A", 0, -3), ("x", 1, 4), ("A", 0, 4), ("A", 0, -4), ("A", 1, 3), ("A", 1, -3),
-    ("P", 1), ("A", 1, 4), ("A", 1, -4),
+    ("L", 0), ("L", 1), ("b", 0, -1), ("b", 0, 1), ("a", 0), ("x", 0, 0), ("b", 0, -2), ("b", 0, 2), ("b", 1, -1),
+    ("b", 1, 1), ("a", 1), ("x", 1, 0), ("x", 0, -1), ("b", 1, -2), ("b", 1, 2), ("x", 0, 1), ("A", 0, -1),
+    ("A", 0, 1), ("x", 0, -2), ("b", 0, -3), ("b", 0, 3), ("x", 0, 2), ("x", 1, -1), ("x", 1, 1), ("b", 0, -4),
+    ("A", 1, 1), ("b", 1, 3), ("A", 1, -1), ("x", 1, -2), ("x", 1, 2), ("b", 1, -3), ("b", 1, 4), ("A", 0, -2),
+    ("x", 0, -3), ("A", 0, 2), ("x", 0, 3), ("P", 0), ("A", 1, 2), ("x", 0, -4), ("A", 1, -2), ("x", 1, 3),
+    ("x", 1, -3), ("A", 0, -3), ("x", 1, 4), ("A", 0, 3), ("A", 0, -4), ("A", 0, 4), ("A", 1, -3), ("A", 1, 3),
+    ("P", 1), ("A", 1, -4), ("A", 1, 4),
 ]
 
 
@@ -199,11 +201,12 @@
     load_tree.wait()
     load_value_up.wait()
 
-    group_heads = head_count // GROUPS
-    group_rows = group_heads * nodes
+    first_head = [sum(GROUP_HEADS[:g]) for g in range(GROUPS)]
 
     def attend(g):
-        q = queries[g * group_rows : (g + 1) * group_rows, :]
+        group_heads = GROUP_HEADS[g]
+        group_rows = group_heads * nodes
+        q = queries[first_head[g] * nodes : first_head[g] * nodes + group_rows, :]
         s = nn_dot(q, keys[...]) * scale + bias
         s_tree = nt_dot(q, tree_rows[...]) * scale + tree_bias[:group_rows]
         peak = jnp.maximum(jnp.max(s, axis=-1, keepdims=True), jnp.max(s_tree, axis=-1, keepdims=True))
@@ -214,18 +217,17 @@
         o = o + nn_dot(e_tree.astype(BF16), tree_rows[:, 0:512])
         o = (o / total).astype(BF16)
         for h in range(group_heads):
-            head = g * group_heads + h
+            head = first_head[g] + h
             done = nn_dot(o[h * nodes : (h + 1) * nodes], value_up[head]).astype(BF16)
             heads[z * 4 + x, :, head * 128 : (head + 1) * 128] = done
 
-    a_width = group_heads * 3 // 8 * 128
-    b_width = group_heads * 128 - a_width
 
     A, B = 0, 1
 
     def columns(part, g):
-        start = g * group_heads * 128 + (0 if part == A else a_width)
-        return pl.ds(start, a_width if part == A else b_width)
+        start = first_head[g] + (0 if part == A else A_HEADS[g])
+        count = A_HEADS[g] if part == A else GROUP_HEADS[g] - A_HEADS[g]
+        return pl.ds(start * 128, count * 128)
 
     def block(part, g, dx, dz):
         return heads.at[((z + dz + 8) % 8) * 4 + (x + dx + 4) % 4, :, columns(part, g)]
@@ -257,6 +259,8 @@
         own = block(B, g, 0, 0)
         go(own, g, "b-1", 0, 1)
         go(own, g, "b1", 0, -1)
+        go(own, g, "b-2", 0, 2)
+        go(own, g, "b2", 0, -2)
         for dx in (1, -1, 2):
             go(block(A, g, 0, 0), g, "a", dx, 0)
         to_x(g, 0)
@@ -271,7 +275,7 @@
         ref = block(B, g, 0, dz)
         arrived(ref, sem_of(g, f"b{dz}"))
         onward = 1 if dz < 0 else -1
-        if abs(dz) <= 2:
+        if abs(dz) == 2:
             go(ref, g, f"b{dz - onward}", 0, onward)
         if abs(dz) == 2 and onward == far_side(B, g):
             go(ref, g, f"b{dz - 2 * onward}", 0, 2 * onward)

time: 55.8 us -> 54.6 us (0.978)
  Pallas kernels: 53.6 us -> 52.4 us
    pallas_call x1, Pallas kernels: 53.6 us -> 52.4 us  [on_device(): pl.pallas_call(kernel, out_shape=jax.ShapeDtypeStruct((64, 224), BF16), i...]
where the time goes in v7:
time: 54.6 us; the launch traced here: 54.4 us
  Pallas kernels  52.4 us (96%)
  local copies, waits for them, and re-layouts  1.38 us (3%)
  between operations  0.66 us (1%)
    pallas_call x1, Pallas kernels, on_device(): pl.pallas_call(kernel, out_shape=jax.ShapeDtypeStruct((64, 224), BF16), i...  52.4 us
    unnamed x1, local copies, waits for them, and re-layouts  1.38 us

profile of v7, /device:TPU:1, one launch (start us, length us, event | category | flops | bytes accessed | tf_op | source)
XLA Modules:
  0.0 54.4 jit_solution(9589459293622202918)
XLA Ops:
  0.7 52.4 %tree_attention.1 = bf16[64,224]{1,0:T(8,128)(2,1)} custom-call(bf16[576,256]{1,0:T(8,128)(2,1)} %bitcast.9, s32[1]{0:T(128)S(6)} %copy.12.length_ref, s32[8]{0:T(128)} %slots_ref.1, s32[1,64]{1,0:T(1,128)} %parents_ref.1, bf16[8,8,16,128]{3,2,1,0:T(8,128)(2,1)} %bitcast.10, bf16[8,8,16,64]{3,2,1,0:T(8,128)(2,1)} %bitcast.11, bf16[64,576]{1,0:T(8,128)(2,1)} %bitcast.13, ...), custom_call_target="tpu_custom_call" | custom-call | tf_op jit(solution)/shard_map/tree_attention/pallas_call | solution.py:363
  53.1 1.4 %copy.13 = bf16[8,8,224]{2,1,0:T(8,128)(2,1)} copy(bf16[8,8,224]{2,1,0:T(8,128)(2,1)} %bitcast.12) | data formatting | bytes 57344

commit v8 on v7

--- a/solution.py
+++ b/solution.py
@@ -24,9 +24,9 @@
     ("b", 1, 1), ("a", 1), ("x", 1, 0), ("x", 0, -1), ("b", 1, -2), ("b", 1, 2), ("x", 0, 1), ("A", 0, -1),
     ("A", 0, 1), ("x", 0, -2), ("b", 0, -3), ("b", 0, 3), ("x", 0, 2), ("x", 1, -1), ("x", 1, 1), ("b", 0, -4),
     ("A", 1, 1), ("b", 1, 3), ("A", 1, -1), ("x", 1, -2), ("x", 1, 2), ("b", 1, -3), ("b", 1, 4), ("A", 0, -2),
-    ("x", 0, -3), ("A", 0, 2), ("x", 0, 3), ("P", 0), ("A", 1, 2), ("x", 0, -4), ("A", 1, -2), ("x", 1, 3),
-    ("x", 1, -3), ("A", 0, -3), ("x", 1, 4), ("A", 0, 3), ("A", 0, -4), ("A", 0, 4), ("A", 1, -3), ("A", 1, 3),
-    ("P", 1), ("A", 1, -4), ("A", 1, 4),
+    ("x", 0, -3), ("A", 0, 2), ("x", 0, 3), ("A", 1, 2), ("x", 0, -4), ("A", 1, -2), ("x", 1, 3), ("x", 1, -3),
+    ("P", 0), ("A", 0, -3), ("x", 1, 4), ("A", 0, 3), ("A", 0, -4), ("A", 0, 4), ("A", 1, -3), ("A", 1, 3), ("P", 1),
+    ("A", 1, -4), ("A", 1, 4),
 ]
 
 
@@ -49,7 +49,7 @@
 def kernel(
     cache_ref, length_ref, slots_ref, parents_ref, nope_ref, rope_ref, latent_ref, key_up_ref, value_up_ref, proj_ref,
     out_ref,
-    slot_ref, raw, live, keys, parents, nope, rope, tree_rows, key_up, value_up, proj, proj_t, queries, heads, partial, sums,
+    slot_ref, raw, live, keys, parents, nope, rope, tree_rows, key_up, value_up, proj, proj_t, queries, heads, partial, sums, totals,
     local_sem, raw_sem, key_sem, head_sem, send_sem,
 ):
     ctx, tp, dec = lax.axis_index("ctx"), lax.axis_index("tp"), lax.axis_index("dec")
@@ -310,7 +310,7 @@
             for other in (False, True):
                 if dy or other:
                     device = at_tp(dy, other)
-                    send(SUMS, partial.at[origin, device[1]], sums.at[origin, tp], raw_sem.at[2], device)
+                    send(SUMS, partial.at[origin, device[1]], sums.at[origin, tp], raw_sem.at[3 if k == 2 else 2], device)
 
     def by_target(r):
         j, rest = r // 16, r % 16
@@ -337,18 +337,20 @@
     opposite("far", 2)
     project(2)
     every = sums.reshape(32, 16, 224)
-    arrived(every.at[pl.ds(0, 28)], raw_sem.at[2])
-    totals = []
-    for origin in range(4):
+    arrived(every.at[pl.ds(0, 21)], raw_sem.at[2])
+    for k in (0, 1, 3, 2):
+        if k == 2:
+            arrived(every.at[pl.ds(0, 7)], raw_sem.at[3])
+        origin = (ctx + k) % 4
         total = jnp.zeros((16, 224), F32)
         for source in range(8):
             total = total + sums[origin, source].astype(F32)
-        totals.append(total.astype(BF16))
+        totals[origin] = total.astype(BF16)
 
     def by_slot(r):
         return ((r // 2) % 4) * 16 + ((r // 8) % 2) * 8 + (r // 16) * 2 + r % 2
 
-    out_ref[...] = permuted(by_slot, jnp.concatenate(totals, axis=0))
+    out_ref[...] = permuted(by_slot, totals[...].reshape(64, 224))
     all_sent(LIVE, live.at[pl.ds(0, 7)])
     all_sent(RAW, raw.at[pl.ds(0, 7)])
     all_sent(KEYS, value_up.reshape(8192, 128).at[pl.ds(0, 31 * 144)])
@@ -382,7 +384,8 @@
             pltpu.VMEM((32, 16, 2048), BF16),
             pltpu.VMEM((4, 8, 16, 224), BF16),
             pltpu.VMEM((4, 8, 16, 224), BF16),
-            dma((9,)), dma((3,)), dma((16,)), dma((GROUPS * len(HEAD_SEMS),)), dma((5,)),
+            pltpu.VMEM((4, 16, 224), BF16),
+            dma((9,)), dma((4,)), dma((16,)), dma((GROUPS * len(HEAD_SEMS),)), dma((5,)),
         ],
         compiler_params=pltpu.CompilerParams(
             collective_id=0, has_side_effects=True, vmem_limit_bytes=58 * 1024 * 1024

time: 54.6 us -> 54.5 us (level)
  no operation moved by 1% of the time
where the time goes in v8:
time: 54.5 us; the launch traced here: 54.4 us
  Pallas kernels  52.4 us (96%)
  local copies, waits for them, and re-layouts  1.38 us (3%)
  between operations  0.66 us (1%)
    pallas_call x1, Pallas kernels, on_device(): pl.pallas_call(kernel, out_shape=jax.ShapeDtypeStruct((64, 224), BF16), i...  52.4 us
    unnamed x1, local copies, waits for them, and re-layouts  1.38 us

profile of v8, /device:TPU:1, one launch (start us, length us, event | category | flops | bytes accessed | tf_op | source)
XLA Modules:
  0.0 54.4 jit_solution(14195063089354416293)
XLA Ops:
  0.7 52.4 %tree_attention.1 = bf16[64,224]{1,0:T(8,128)(2,1)} custom-call(bf16[576,256]{1,0:T(8,128)(2,1)} %bitcast.9, s32[1]{0:T(128)S(6)} %copy.12.length_ref, s32[8]{0:T(128)} %slots_ref.1, s32[1,64]{1,0:T(1,128)} %parents_ref.1, bf16[8,8,16,128]{3,2,1,0:T(8,128)(2,1)} %bitcast.10, bf16[8,8,16,64]{3,2,1,0:T(8,128)(2,1)} %bitcast.11, bf16[64,576]{1,0:T(8,128)(2,1)} %bitcast.13, ...), custom_call_target="tpu_custom_call" | custom-call | tf_op jit(solution)/shard_map/tree_attention/pallas_call | solution.py:365
  53.0 1.4 %copy.13 = bf16[8,8,224]{2,1,0:T(8,128)(2,1)} copy(bf16[8,8,224]{2,1,0:T(8,128)(2,1)} %bitcast.12) | data formatting | bytes 57344

commit v9 on v8

--- a/solution.py
+++ b/solution.py
@@ -75,9 +75,7 @@
 
     peers = [at_dec(k) for k in range(1, 8)]
     peers += [at_ctx(k) for k in range(1, 4)]
-    peers += [at_tp(dy) for dy in (1, 2, 3)] + [at_tp(dy, True) for dy in range(4)]
-    away = (z + 7 + 2 * z_lo) % 8
-    peers.append((away // 2, tp, x * 2 + away % 2))
+    peers += [at_tp(dy) for dy in (1, 2, 3)] + [at_tp(0, True)]
 
     LIVE, RAW, KEYS, HEADS, SUMS = range(5)
 
@@ -215,7 +213,7 @@
         total = jnp.sum(e, axis=-1, keepdims=True) + jnp.sum(e_tree, axis=-1, keepdims=True)
         o = nt_dot(e.astype(BF16), keys[0:512, :])
         o = o + nn_dot(e_tree.astype(BF16), tree_rows[:, 0:512])
-        o = (o / total).astype(BF16)
+        o = (o * (1.0 / total)).astype(BF16)
         for h in range(group_heads):
             head = first_head[g] + h
             done = nn_dot(o[h * nodes : (h + 1) * nodes], value_up[head]).astype(BF16)

time: 54.5 us -> 54.5 us (level)
  no operation moved by 1% of the time
where the time goes in v9:
time: 54.5 us; the launch traced here: 54.4 us
  Pallas kernels  52.4 us (96%)
  local copies, waits for them, and re-layouts  1.38 us (3%)
  between operations  0.66 us (1%)
    pallas_call x1, Pallas kernels, on_device(): pl.pallas_call(kernel, out_shape=jax.ShapeDtypeStruct((64, 224), BF16), i...  52.4 us
    unnamed x1, local copies, waits for them, and re-layouts  1.38 us

profile of v9, /device:TPU:1, one launch (start us, length us, event | category | flops | bytes accessed | tf_op | source)
XLA Modules:
  0.0 54.4 jit_solution(1006578202190194813)
XLA Ops:
  0.7 52.4 %tree_attention.1 = bf16[64,224]{1,0:T(8,128)(2,1)} custom-call(bf16[576,256]{1,0:T(8,128)(2,1)} %bitcast.9, s32[1]{0:T(128)S(6)} %copy.12.length_ref, s32[8]{0:T(128)} %slots_ref.1, s32[1,64]{1,0:T(1,128)} %parents_ref.1, bf16[8,8,16,128]{3,2,1,0:T(8,128)(2,1)} %bitcast.10, bf16[8,8,16,64]{3,2,1,0:T(8,128)(2,1)} %bitcast.11, bf16[64,576]{1,0:T(8,128)(2,1)} %bitcast.13, ...), custom_call_target="tpu_custom_call" | custom-call | tf_op jit(solution)/shard_map/tree_attention/pallas_call | solution.py:363
  53.0 1.4 %copy.13 = bf16[8,8,224]{2,1,0:T(8,128)(2,1)} copy(bf16[8,8,224]{2,1,0:T(8,128)(2,1)} %bitcast.12) | data formatting | bytes 57344
